TPU v7x, 512 devices: a whole 4x8x8 slice. The times are simulated.
512 devices in a mesh: dp: 64 (over z_hi, y, core), seq: 8 (over z_lo, x).
Axes of the slice: x: 4, y: 8, z: 8 (z_hi: 4, z_lo: 2; z = z_hi * 2 + z_lo), core: 2. Of those that a mesh axis runs over, the one named last changes fastest.
Arguments:
- query_rows: bfloat16 [64, 1536, 2048], P('dp', 'seq'), may hold values from -6 to 6
- key_rows: bfloat16 [64, 1536, 2048], P('dp', 'seq'), may hold values from -6 to 6
- value_rows: bfloat16 [64, 1536, 2048], P('dp', 'seq'), may hold values from -6 to 6
- key_tiles: int32 [16, 4, 4], replicated, may hold values from 0 to 3, as said below
- tile_counts: int32 [16, 4], replicated, may hold values from 1 to 4
- out_weight: bfloat16 [2048, 3072], P('dp'), may hold values from -1.25 to 1.25
- gate_scale: bfloat16 [64, 3072], P('dp'), may hold values from 0.5 to 1.5
- residual: bfloat16 [64, 1536, 3072], P('dp', 'seq'), may hold values from -6 to 6
Outputs:
- block_out: bfloat16 [64, 1536, 3072], P('dp', 'seq')
Inputs may be any that keep to these rules, and one draw needn't show every extreme that they name: Tiles form a grid of 2 frame positions by 2 height positions by 1 width positions; the tile at frame index a, height index b and width index c has the number a * 2 + b + c. The first tile_counts[h, s] entries of key_tiles[h, s, :] are, in increasing order, the distinct tiles of a box of this grid that contains tile s; the remaining entries equal s.
All inputs are finite; a program needn't handle non-finite values.
Results may differ from a plain program's by a relative error of at most 0.012.
Values may be sent and summed in bfloat16 or wider, within the bound.
A program may use at most 64 MiB of HBM per device.

v0:
```python
import math

import jax
import jax.numpy as jnp
from jax import lax
from jax.sharding import PartitionSpec as P


def slot_scores(query_blocks, key_blocks, value_blocks, head_tiles, slot_index, scale):
    chosen = lax.dynamic_index_in_dim(head_tiles, slot_index, 1, keepdims=False)
    near_keys = jnp.take(key_blocks, chosen, axis=0)
    near_values = jnp.take(value_blocks, chosen, axis=0)
    scores = (
        jnp.einsum("tqd,tkd->tqk", query_blocks, near_keys, preferred_element_type=jnp.float32)
        * scale
    )
    return (scores, near_values)


def attend_head(query_blocks, key_blocks, value_blocks, head_tiles, head_counts, scale):
    scores, near_values = slot_scores(query_blocks, key_blocks, value_blocks, head_tiles, 0, scale)
    row_peak = jnp.max(scores, axis=2)
    weights = jnp.exp(scores - row_peak[:, :, None])
    row_total = jnp.sum(weights, axis=2)
    running = jnp.einsum(
        "tqk,tkd->tqd",
        weights.astype(jnp.bfloat16),
        near_values,
        preferred_element_type=jnp.float32,
    )

    def one_slot(slot_index, carry):
        row_peak, row_total, running = carry
        scores, near_values = slot_scores(
            query_blocks, key_blocks, value_blocks, head_tiles, slot_index, scale
        )
        active = (slot_index < head_counts)[:, None]
        new_peak = jnp.where(active, jnp.maximum(row_peak, jnp.max(scores, axis=2)), row_peak)
        weights = jnp.where(active[:, :, None], jnp.exp(scores - new_peak[:, :, None]), 0.0)
        rescale = jnp.exp(row_peak - new_peak)
        row_total = row_total * rescale + jnp.sum(weights, axis=2)
        running = running * rescale[:, :, None] + jnp.einsum(
            "tqk,tkd->tqd",
            weights.astype(jnp.bfloat16),
            near_values,
            preferred_element_type=jnp.float32,
        )
        return (new_peak, row_total, running)

    last_slot = jnp.max(head_counts)
    row_peak, row_total, running = lax.fori_loop(
        1, last_slot, one_slot, (row_peak, row_total, running)
    )
    return (running / row_total[:, :, None]).astype(jnp.bfloat16)


def head_blocks(rows, first_col, head_dim, ntiles, tile_len):
    return rows[:, first_col : first_col + head_dim].reshape(ntiles, tile_len, head_dim)


def on_device(
    query_rows, key_rows, value_rows, key_tiles, tile_counts, out_weight, gate_scale, residual
):
    groups = lax.axis_size("seq")
    seq_index = lax.axis_index("seq")
    tok_rows = query_rows.shape[1]
    feat_width = query_rows.shape[2]
    head_count = key_tiles.shape[0]
    ntiles = key_tiles.shape[1]
    head_dim = feat_width // head_count
    local_heads = head_count // groups
    seqlen = tok_rows * groups
    tile_len = seqlen // ntiles
    scale = 1.0 / math.sqrt(head_dim)
    queries = query_rows[0]
    keys_here = key_rows[0]
    values_here = value_rows[0]
    assign = jnp.arange(head_count, dtype=jnp.int32)
    heads_query, heads_key, heads_value = (
        lax.all_to_all(queries, "seq", split_axis=1, concat_axis=0, tiled=True),
        lax.all_to_all(keys_here, "seq", split_axis=1, concat_axis=0, tiled=True),
        lax.all_to_all(values_here, "seq", split_axis=1, concat_axis=0, tiled=True),
    )
    outputs = []
    for slot_head in range(local_heads):
        global_head = assign[seq_index * local_heads + slot_head]
        head_tiles = lax.dynamic_index_in_dim(key_tiles, global_head, 0, keepdims=False)
        head_counts = lax.dynamic_index_in_dim(tile_counts, global_head, 0, keepdims=False)
        first_col = slot_head * head_dim
        mixed_head = attend_head(
            head_blocks(heads_query, first_col, head_dim, ntiles, tile_len),
            head_blocks(heads_key, first_col, head_dim, ntiles, tile_len),
            head_blocks(heads_value, first_col, head_dim, ntiles, tile_len),
            head_tiles,
            head_counts,
            scale,
        )
        outputs.append(mixed_head.reshape(seqlen, head_dim))
    attended = jnp.concatenate(outputs, axis=1)
    token_major = lax.all_to_all(attended, "seq", split_axis=0, concat_axis=1, tiled=True)
    projected = jnp.dot(
        token_major,
        lax.all_gather(out_weight, "dp", axis=0, tiled=True),
        preferred_element_type=jnp.float32,
    )
    block_out = (
        residual[0].astype(jnp.float32) + gate_scale[0].astype(jnp.float32)[None, :] * projected
    )
    return block_out.astype(jnp.bfloat16)[None]


def solution(mesh):
    in_specs = (
        P("dp", "seq", None),
        P("dp", "seq", None),
        P("dp", "seq", None),
        P(),
        P(),
        P("dp", None),
        P("dp", None),
        P("dp", "seq", None),
    )
    out_specs = P("dp", "seq", None)
    return jax.shard_map(
        on_device, mesh=mesh, in_specs=in_specs, out_specs=out_specs, check_vma=False
    )
```

profile of v0, /device:TPU:48, one launch (start us, length us, event | category | flops | bytes accessed | tf_op | source)
XLA Modules:
  0.0 171.7 jit_solution(16815847340062318840)
XLA Ops:
  6.5 0.7 all-gather.2.cloned.1.call-update
  7.3 1.4 copy.53
  8.7 1.0 copy.38
  9.7 6.1 %all-to-all-start = ((bf16[192,8,256]{2,0,1:T(8,128)(2,1)}), bf16[192,8,256]{2,0,1:T(8,128)(2,1)S(1)}, u32[]{:S(2)}, u32[]{:S(2)}) async-start(bf16[192,8,256]{2,0,1:T(8,128)(2,1)} %copy.38), calls=%async_computation | async-start | bytes 1572864 | tf_op jit(solution)/shard_map/all_to_all | solution.py:81
  16.0 1.1 copy.40
  17.1 10.7 %all-to-all-done = bf16[192,8,256]{2,0,1:T(8,128)(2,1)S(1)} async-done(((bf16[192,8,256]{2,0,1:T(8,128)(2,1)}), bf16[192,8,256]{2,0,1:T(8,128)(2,1)S(1)}, u32[]{:S(2)}, u32[]{:S(2)}) %all-to-all-start) | async-done | bytes 786464 | tf_op jit(solution)/shard_map/all_to_all | solution.py:81
  27.8 3.6 %all-to-all-start.2 = ((bf16[192,8,256]{2,0,1:T(8,128)(2,1)}), bf16[192,8,256]{2,0,1:T(8,128)(2,1)S(1)}, u32[]{:S(2)}, u32[]{:S(2)}) async-start(bf16[192,8,256]{2,0,1:T(8,128)(2,1)} %copy.40), calls=%async_computation.2 | async-start | bytes 1572864 | tf_op jit(solution)/shard_map/all_to_all | solution.py:82
  31.6 1.0 copy.39
  32.8 0.7 copy.50
  33.4 0.7 copy.51
  34.1 0.8 dynamic-slice_reduce_fusion.4
  35.3 12.3 %all-to-all-done.2 = bf16[192,8,256]{2,0,1:T(8,128)(2,1)S(1)} async-done(((bf16[192,8,256]{2,0,1:T(8,128)(2,1)}), bf16[192,8,256]{2,0,1:T(8,128)(2,1)S(1)}, u32[]{:S(2)}, u32[]{:S(2)}) %all-to-all-start.2) | async-done | bytes 786464 | tf_op jit(solution)/shard_map/all_to_all | solution.py:82
  47.6 4.5 %all-to-all-start.1 = ((bf16[192,8,256]{2,0,1:T(8,128)(2,1)}), bf16[192,8,256]{2,0,1:T(8,128)(2,1)S(1)}, u32[]{:S(2)}, u32[]{:S(2)}) async-start(bf16[192,8,256]{2,0,1:T(8,128)(2,1)} %copy.39), calls=%async_computation.1 | async-start | bytes 1572864 | tf_op jit(solution)/shard_map/all_to_all | solution.py:80
  52.1 0.8 fusion.78
  52.9 1.8 %gather_fusion.4 = bf16[4,384,128]{2,1,0:T(8,128)(2,1)S(1)} fusion(bf16[4,384,128]{2,1,0:T(8,128)(2,1)} %bitcast.8, s32[1024]{0:T(1024)S(1)} %pad_clamp_fusion.3), kind=kCustom, calls=%fused_computation.clone | custom fusion | bytes 786448 | tf_op jit(solution)/shard_map/jit(_take)/gather | solution.py:11
  54.7 0.8 fusion.77
  55.5 1.8 %gather_fusion.5 = bf16[4,384,128]{2,1,0:T(8,128)(2,1)S(1)} fusion(bf16[4,384,128]{2,1,0:T(8,128)(2,1)} %bitcast.15, s32[1024]{0:T(1024)S(1)} %pad_clamp_fusion.3), kind=kCustom, calls=%fused_computation.2.clone | custom fusion | bytes 786448 | tf_op jit(solution)/shard_map/jit(_take)/gather | solution.py:12
  57.2 0.6 gather_fusion.6
  57.9 1.3 gather_fusion.7
  59.2 4.8 %all-to-all-done.1 = bf16[192,8,256]{2,0,1:T(8,128)(2,1)S(1)} async-done(((bf16[192,8,256]{2,0,1:T(8,128)(2,1)}), bf16[192,8,256]{2,0,1:T(8,128)(2,1)S(1)}, u32[]{:S(2)}, u32[]{:S(2)}) %all-to-all-start.1) | async-done | bytes 786464 | tf_op jit(solution)/shard_map/all_to_all | solution.py:80
  64.1 0.5 bitcast_reduce_fusion.3
  64.6 1.0 fusion.46
  66.1 1.4 copy-done
  67.5 1.0 fusion.48
  68.5 1.6 fusion.51
  70.1 12.0 %while.28 = (s32[]{:T(128)}, f32[4,384]{1,0:T(4,128)S(1)}, f32[4,384]{1,0:T(4,128)}, f32[4,384,128]{2,1,0:T(8,128)}, s32[]{:T(128)}, /*index=5*/s32[4]{0:T(128)}...) while((s32[]{:T(128)}, f32[4,384]{1,0:T(4,128)S(1)}, ...), condition=%wide.region_6.9_spmd, body=%wide.region_3.8_spmd.sunk | while | flops 308680224 | bytes 11620871 | solution.py:51
  70.8 1.3 compare_and_fusion.6
  72.1 1.6 gather_fusion
  73.7 0.5 bitcast_reduce_fusion.6
  74.4 0.8 maximum_select_fusion.4
  75.6 0.6 multiply_add_fusion.4
  76.2 0.6 copy-done.12
  76.8 1.7 %gather_fusion.1 = bf16[4,384,128]{2,1,0:T(8,128)(2,1)S(1)} fusion(bf16[4,384,128]{2,1,0:T(8,128)(2,1)} %get-tuple-element.501, s32[1024]{0:T(1024)} %copy-done.13), kind=kCustom, calls=%fused_computation.5.clone.clone.1 | custom fusion | bytes 786448 | tf_op jit(solution)/shard_map/while/body/jit(_take)/gather | solution.py:12
  78.6 2.8 %convolution_add_fusion.4 = f32[4,384,128]{2,1,0:T(8,128)} fusion(f32[4,384,384]{2,1,0:T(8,128)S(1)} %get-tuple-element.407, f32[4,384]{1,0:T(4,128)S(1)} %maximum_select_fusion.4, pred[4]{0:T(512)(128)(4,1)} %get-tuple-element.406, f32[4,384,128]{2,1,0:T(8,128)} %get-tuple-element.482, bf16[4,384,128]{2,1,0:T(8,128)(2,1)S(1)} %gather_fusion.1, ...), kind=kOutput, calls=%fused_computation.14.clone.1 | convolution fusion | flops 153944064 | bytes 4337672 | tf_op jit(solution)/shard_map/while/body/tqk,tkd->tqd/dot_general | solution.py:42
  82.1 2.2 %divide_convert_fusion.1 = bf16[4,384,128]{2,1,0:T(8,128)(2,1)} fusion(f32[4,384,128]{2,1,0:T(8,128)} %get-tuple-element.115, f32[4,384]{1,0:T(4,128)} %get-tuple-element.116), kind=kLoop, calls=%fused_computation.88 | loop fusion | flops 393216 | bytes 1185792 | tf_op jit(solution)/shard_map/convert_element_type | solution.py:54
  84.3 3.4 %fusion.49 = f32[4,384,128]{2,1,0:T(8,128)} fusion(f32[4,384,384]{2,1,0:T(8,128)} %copy-done, f32[4,384]{1,0:T(4,128)S(1)} %get-tuple-element.428, bf16[4,384,128]{2,1,0:T(8,128)(2,1)} %gather_fusion.7, pred[4]{0:T(512)(128)(4,1)} %copy-done.22), kind=kOutput, calls=%fused_computation.80 | convolution fusion | flops 152961024 | bytes 3545092 | tf_op jit(solution)/shard_map/tqk,tkd->tqd/dot_general | solution.py:25
  87.7 10.1 %while.29 = (s32[]{:T(128)}, f32[4,384]{1,0:T(4,128)S(1)}, f32[4,384]{1,0:T(4,128)}, f32[4,384,128]{2,1,0:T(8,128)}, s32[]{:T(128)}, /*index=5*/s32[4]{0:T(128)}...) while((s32[]{:T(128)}, f32[4,384]{1,0:T(4,128)S(1)}, ...), condition=%wide.region_13.16_spmd, body=%wide.region_10.15_spmd.sunk | while | flops 308680224 | bytes 13144555 | solution.py:51
  88.4 1.2 compare_and_fusion.7
  89.6 0.6 gather_fusion.2
  91.5 0.6 multiply_add_fusion.5
  92.1 0.6 copy-done.10
  92.7 1.5 gather_fusion.3
  94.1 3.0 %convolution_add_fusion.5 = f32[4,384,128]{2,1,0:T(8,128)} fusion(f32[4,384,384]{2,1,0:T(8,128)S(1)} %get-tuple-element.424, f32[4,384]{1,0:T(4,128)S(1)} %maximum_select_fusion.5, pred[4]{0:T(512)(128)(4,1)} %get-tuple-element.423, f32[4,384,128]{2,1,0:T(8,128)} %get-tuple-element.443, bf16[4,384,128]{2,1,0:T(8,128)(2,1)} %gather_fusion.3, ...), kind=kOutput, calls=%fused_computation.43.clone.1 | convolution fusion | flops 153944064 | bytes 4337672 | tf_op jit(solution)/shard_map/while/body/tqk,tkd->tqd/dot_general | solution.py:42
  97.8 1.4 divide_convert_fusion
  99.3 2.1 %pad_maximum_fusion = bf16[8,192,256]{2,1,0:T(8,128)(2,1)} fusion(bf16[8,192,128]{2,1,0:T(8,128)(2,1)S(1)} %bitcast.125, bf16[8,192,128]{2,1,0:T(8,128)(2,1)} %bitcast.124), kind=kLoop, calls=%fused_computation.86 | loop fusion | flops 1572864 | bytes 1572864 | tf_op jit(solution)/shard_map/concatenate | solution.py:99
  101.3 43.8 %all-to-all-start.3 = ((bf16[8,192,256]{2,1,0:T(8,128)(2,1)}), bf16[8,192,256]{2,1,0:T(8,128)(2,1)S(1)}, u32[]{:S(2)}, u32[]{:S(2)}) async-start(bf16[8,192,256]{2,1,0:T(8,128)(2,1)} %pad_maximum_fusion), calls=%async_computation.3 | async-start | bytes 1572864 | tf_op jit(solution)/shard_map/all_to_all | solution.py:100
  145.2 11.3 %all-to-all-done.3 = bf16[8,192,256]{2,1,0:T(8,128)(2,1)S(1)} async-done(((bf16[8,192,256]{2,1,0:T(8,128)(2,1)}), bf16[8,192,256]{2,1,0:T(8,128)(2,1)S(1)}, u32[]{:S(2)}, u32[]{:S(2)}) %all-to-all-start.3) | async-done | bytes 786464 | tf_op jit(solution)/shard_map/all_to_all | solution.py:100
  156.6 8.2 %fusion.42 = bf16[1,192,3072]{2,1,0:T(8,128)(2,1)} fusion(bf16[192,2048]{1,0:T(8,128)(2,1)S(1)} %bitcast.129, bf16[2048,3072]{1,0:T(8,128)(2,1)} %all-gather.2.cloned.1.call-done, bf16[1,192,3072]{2,1,0:T(8,128)(2,1)S(1)} %copy-done.23, f32[3072]{0:T(1024)S(1)} %bitcast.130), kind=kOutput, calls=%fused_computation.69 | convolution fusion | flops 2418278400 | bytes 15740928 | tf_op jit(solution)/shard_map/dot_general | solution.py:101
  (67 shorter events, 3.3 us)
Async XLA Ops:
  6.5 150.0 %all-gather.2.cloned.1.call-start = ((), (), s32[]{:S(2)}) async-start(), calls=%async_computation.4 | async-start | bytes 12779520 | tf_op jit(solution)/shard_map/all_gather | solution.py:103
  7.3 8.6 %copy-start.7 = (bf16[1,192,2048]{2,1,0:T(8,128)(2,1)S(1)}, bf16[1,192,2048]{2,1,0:T(8,128)(2,1)}, u32[]{:S(2)}) copy-start(bf16[1,192,2048]{2,1,0:T(8,128)(2,1)} %param.18) | copy-start | bytes 2359300
  9.7 18.1 %all-to-all-start = ((bf16[192,8,256]{2,0,1:T(8,128)(2,1)}), bf16[192,8,256]{2,0,1:T(8,128)(2,1)S(1)}, u32[]{:S(2)}, u32[]{:S(2)}) async-start(bf16[192,8,256]{2,0,1:T(8,128)(2,1)} %copy.38), calls=%async_computation | async-start | bytes 1572864 | tf_op jit(solution)/shard_map/all_to_all | solution.py:81
  15.8 15.6 %copy-start.8 = (bf16[1,192,2048]{2,1,0:T(8,128)(2,1)S(1)}, bf16[1,192,2048]{2,1,0:T(8,128)(2,1)}, u32[]{:S(2)}) copy-start(bf16[1,192,2048]{2,1,0:T(8,128)(2,1)} %param.16) | copy-start | bytes 2359300
  17.1 15.6 %copy-start.19 = (s32[16,4,4]{0,2,1:T(4,128)S(1)}, s32[16,4,4]{0,2,1:T(4,128)}, u32[]{:S(2)}) copy-start(s32[16,4,4]{0,2,1:T(4,128)} %param.19) | copy-start | bytes 3076
  17.1 17.0 %copy-start.21 = (s32[16,4]{0,1:T(4,128)S(1)}, s32[16,4]{0,1:T(4,128)}, u32[]{:S(2)}) copy-start(s32[16,4]{0,1:T(4,128)} %param.20) | copy-start | bytes 772
  27.8 19.8 %all-to-all-start.2 = ((bf16[192,8,256]{2,0,1:T(8,128)(2,1)}), bf16[192,8,256]{2,0,1:T(8,128)(2,1)S(1)}, u32[]{:S(2)}, u32[]{:S(2)}) async-start(bf16[192,8,256]{2,0,1:T(8,128)(2,1)} %copy.40), calls=%async_computation.2 | async-start | bytes 1572864 | tf_op jit(solution)/shard_map/all_to_all | solution.py:82
  47.6 16.4 %all-to-all-start.1 = ((bf16[192,8,256]{2,0,1:T(8,128)(2,1)}), bf16[192,8,256]{2,0,1:T(8,128)(2,1)S(1)}, u32[]{:S(2)}, u32[]{:S(2)}) async-start(bf16[192,8,256]{2,0,1:T(8,128)(2,1)} %copy.39), calls=%async_computation.1 | async-start | bytes 1572864 | tf_op jit(solution)/shard_map/all_to_all | solution.py:80
  52.1 13.5 %copy-start.22 = (pred[4]{0:T(512)(128)(4,1)}, pred[4]{0:T(512)(128)(4,1)S(1)}, u32[]{:S(2)}) copy-start(pred[4]{0:T(512)(128)(4,1)S(1)} %get-tuple-element.273) | copy-start | bytes 16
  52.9 6.3 %copy-start.1 = (bf16[1536,128]{1,0:T(8,128)(2,1)}, bf16[1536,128]{1,0:T(8,128)(2,1)S(1)}, u32[]{:S(2)}) copy-start(bf16[1536,128]{1,0:T(8,128)(2,1)S(1)} %get-tuple-element.262) | copy-start | bytes 1179652
  55.5 8.5 %copy-start.3 = (bf16[1536,128]{1,0:T(8,128)(2,1)}, bf16[1536,128]{1,0:T(8,128)(2,1)S(1)}, u32[]{:S(2)}) copy-start(bf16[1536,128]{1,0:T(8,128)(2,1)S(1)} %get-tuple-element.260) | copy-start | bytes 1179652
  66.1 1.4 copy-start
  70.7 1.3 copy-start.5
  72.0 2.2 %copy-start.17 = (pred[4]{0:T(512)(128)(4,1)}, pred[4]{0:T(512)(128)(4,1)S(1)}, u32[]{:S(2)}) copy-start(pred[4]{0:T(512)(128)(4,1)S(1)} %get-tuple-element.404) | copy-start | bytes 16 | tf_op jit(solution)/shard_map/while
  72.0 2.2 %copy-start.13 = (s32[1024]{0:T(1024)}, s32[1024]{0:T(1024)S(1)}, u32[]{:S(2)}) copy-start(s32[1024]{0:T(1024)S(1)} %pad_clamp_fusion.6) | copy-start | bytes 12292 | tf_op jit(solution)/shard_map/while
  73.7 0.7 copy-start.15
  73.7 1.9 %copy-start.11 = (f32[4,384]{1,0:T(4,128)S(1)}, f32[4,384]{1,0:T(4,128)}, u32[]{:S(2)}) copy-start(f32[4,384]{1,0:T(4,128)} %get-tuple-element.481) | copy-start | bytes 18436 | tf_op jit(solution)/shard_map/while
  74.2 1.4 copy-start.6
  76.2 0.6 copy-start.12
  82.1 5.6 %copy-start.2 = (bf16[1536,128]{1,0:T(8,128)(2,1)S(1)}, bf16[1536,128]{1,0:T(8,128)(2,1)}, u32[]{:S(2)}) copy-start(bf16[1536,128]{1,0:T(8,128)(2,1)} %copy-done.1) | copy-start | bytes 1179652
  89.6 1.2 copy-start.18
  89.6 1.2 copy-start.14
  90.3 0.6 copy-start.16
  90.3 1.2 copy-start.9
  90.8 1.9 %copy-start.4 = (bf16[4,384,128]{2,1,0:T(8,128)(2,1)S(1)}, bf16[4,384,128]{2,1,0:T(8,128)(2,1)}, u32[]{:S(2)}) copy-start(bf16[4,384,128]{2,1,0:T(8,128)(2,1)} %get-tuple-element.462) | copy-start | bytes 1179652 | tf_op jit(solution)/shard_map/while
  92.1 0.6 copy-start.10
  97.8 47.4 %copy-start.20 = (bf16[1,3072]{1,0:T(2,128)(2,1)S(1)}, bf16[1,3072]{1,0:T(2,128)(2,1)}, u32[]{:S(2)}) copy-start(bf16[1,3072]{1,0:T(2,128)(2,1)} %param.22) | copy-start | bytes 18436
  99.2 57.3 %copy-start.23 = (bf16[1,192,3072]{2,1,0:T(8,128)(2,1)S(1)}, bf16[1,192,3072]{2,1,0:T(8,128)(2,1)}, u32[]{:S(2)}) copy-start(bf16[1,192,3072]{2,1,0:T(8,128)(2,1)} %param.23) | copy-start | bytes 3538948
  101.3 55.1 %all-to-all-start.3 = ((bf16[8,192,256]{2,1,0:T(8,128)(2,1)}), bf16[8,192,256]{2,1,0:T(8,128)(2,1)S(1)}, u32[]{:S(2)}, u32[]{:S(2)}) async-start(bf16[8,192,256]{2,1,0:T(8,128)(2,1)} %pad_maximum_fusion), calls=%async_computation.3 | async-start | bytes 1572864 | tf_op jit(solution)/shard_map/all_to_all | solution.py:100
Sparse Core Ops, SparseCore 0:
  10.6 125.0 all-gather.1
where the time goes:
time: 173 us; the launch traced here: 172 us
  starting transfers between devices  58.1 us (34%)
  waiting for transfers between devices  39.8 us (23%)
  local copies, waits for them, and re-layouts  22.2 us (13%)
  matrix products  21.1 us (12%)
  other arithmetic  14.1 us (8%)
  between operations  13.6 us (8%)
  loops' own time  2.88 us (2%)
    all_to_all x1, starting transfers between devices, on_device(): lax.all_to_all(attended, 'seq', split_axis=0, concat_axis=1, tiled=True)  43.8 us
    all_to_all x1, waiting for transfers between devices, on_device(): lax.all_to_all(values_here, 'seq', split_axis=1, concat_axis=0, tiled=True)  12.3 us
    all_to_all x1, waiting for transfers between devices, on_device(): lax.all_to_all(attended, 'seq', split_axis=0, concat_axis=1, tiled=True)  11.3 us
    all_to_all x1, waiting for transfers between devices, on_device(): lax.all_to_all(keys_here, 'seq', split_axis=1, concat_axis=0, tiled=True)  10.7 us
    dot_general x1, matrix products, on_device(): jnp.dot(token_major, lax.all_gather(out_weight, 'dp', axis=0, tiled=True)...  8.25 us
    gather x4, local copies, waits for them, and re-layouts, slot_scores(): near_values = jnp.take(value_blocks, chosen, axis=0)  6.32 us
    all_to_all x1, starting transfers between devices, on_device(): lax.all_to_all(keys_here, 'seq', split_axis=1, concat_axis=0, tiled=True)  6.11 us
    dot_general x2, matrix products, one_slot(): jnp.einsum('tqk,tkd->tqd', weights.astype(jnp.bfloat16), near_values, pre...  5.81 us
  transfers between devices with their start and end apart: 5, of which 4 were waited for; matrix products, arithmetic and copies ran while one was open for 27% of the time, Pallas kernels for 0%

commit v1 on v0

v1 whole, which is shorter than its diff:
```python
import functools
import math

import jax
import jax.numpy as jnp
from jax import lax
from jax.experimental import pallas as pl
from jax.experimental.pallas import tpu as pltpu
from jax.sharding import PartitionSpec as P

MESH = pl.DeviceIdType.MESH

HEAD_DIM = 128
NX, NZ_LO = 4, 2
NY, NZ_HI, NCORE = 8, 4, 2
GROUP = NX * NZ_LO
SLOTS = 2
NTILES = 4
SHARED = 384
STEPS = ((4, 3, 4, 3), (3, 4, 3, 4))
ARRIVALS = tuple(
    tuple(
        (j, t) for pair in ((0, 1), (2, 3)) for t in range(4) for j in pair if t < STEPS[way][j]
    )
    for way in range(2)
)


def kernel(
    q_in, k_in, v_in, tiles, counts, w_in, gate_in, res_in, out,
    qb, kb, vb, stage, ob, wb, rb, gs, gb, outv,
    a_send, a_recv, a_loc, o_send, o_recv, o_loc, f_send, f_recv,
    y_send, y_recv, b_send, b_recv, z_send, z_recv, s_send, s_recv, s_loc, p_send, p_recv, p_loc,
):
    dp, me = lax.axis_index("dp"), lax.axis_index("seq")
    z_hi, y, core = dp // (NY * NCORE), (dp // NCORE) % NY, dp % NCORE
    z_lo, x = me // NX, me % NX
    way_z = 2 * z_lo - 1
    tok = q_in.shape[1]
    half = w_in.shape[1] // 2
    w_rows = w_in.shape[0]
    other = 1 - core

    sib = (dp + 1 - 2 * core, me)
    ring = tuple(
        (z_hi * NY * NCORE + ((y + d) % NY) * NCORE + core, me) for d in (1, NY - 1)
    )
    near = (((z_hi + way_z + NZ_HI) % NZ_HI) * NY * NCORE + y * NCORE + core, (1 - z_lo) * NX + x)
    twin = (dp, (1 - z_lo) * NX + x)

    def peer(i):
        return ((z_lo + i // NX) % NZ_LO) * NX + (x + i) % NX

    def block_at(zh, yy):
        return ((yy // 2) % 2) * 16 + (zh * 2 + yy // 4) * 2 + yy % 2

    def remote(src, dst, send, recv, to):
        return pltpu.make_async_remote_copy(
            src_ref=src, dst_ref=dst, send_sem=send, recv_sem=recv, device_id=to, device_id_type=MESH
        )

    def head_cols(p, slot):
        return pl.ds(pl.multiple_of((p * SLOTS + slot) * HEAD_DIM, HEAD_DIM), HEAD_DIM)

    mine = pl.ds(pl.multiple_of(core * half, 128), half)
    theirs = pl.ds(pl.multiple_of(other * half, 128), half)
    orders = tuple(
        (z_hi + NZ_HI + off) % NZ_HI for off in (0, way_z, -way_z, 2)
    )
    y_cols = pl.ds(pl.multiple_of(z_lo * SHARED, 128), half - SHARED)
    b_cols = pl.ds(pl.multiple_of(z_lo * (half - SHARED), 128), SHARED)
    b_cols_in = pl.ds(pl.multiple_of((1 - z_lo) * (half - SHARED), 128), SHARED)
    own_block = block_at(z_hi, y)

    w_local = pltpu.make_async_copy(
        w_in.at[:, mine], wb.at[own_block, pl.ds(core * w_rows, w_rows)], s_loc.at[0]
    )
    w_local.start()
    tensors = ((k_in, kb), (q_in, qb), (v_in, vb))

    def own_copy(n, slot):
        src, dst = tensors[n]
        return pltpu.make_async_copy(src.at[0, :, head_cols(me, slot)], dst.at[slot, me], a_loc.at[n, slot])

    for slot in range(SLOTS):
        for n in range(3):
            own_copy(n, slot).start()
    r_local = pltpu.make_async_copy(res_in.at[0, :, mine], rb.at[core], s_loc.at[1])
    r_local.start()
    gs[...] = jnp.broadcast_to(gate_in[...].astype(jnp.float32), gs.shape)
    g_local = pltpu.make_async_copy(gs.at[:, mine], gb.at[core], s_loc.at[2])
    g_local.start()

    barrier = pltpu.get_barrier_semaphore()
    for to in (sib, *ring, near):
        pl.semaphore_signal(barrier, inc=1, device_id=to, device_id_type=MESH)

    def greet(i, _):
        pl.semaphore_signal(barrier, inc=1, device_id=(dp, peer(i)), device_id_type=MESH)
        return 0

    lax.fori_loop(1, GROUP, greet, 0)
    pl.semaphore_wait(barrier, GROUP + 3)

    w_sib = remote(
        w_in.at[:, theirs],
        wb.at[own_block, pl.ds(core * w_rows, w_rows)],
        s_send.at[0], s_recv.at[0], sib,
    )
    w_sib.start()

    def send_copy(n, slot, p):
        src, dst = tensors[n]
        return remote(
            src.at[0, :, head_cols(p, slot)], dst.at[slot, me],
            a_send.at[n, slot, p], a_recv.at[n, slot, me], (dp, p),
        )

    def arrival(n, slot, p):
        src, dst = tensors[n]
        return remote(
            src.at[0, :, head_cols(p, slot)], dst.at[slot, p],
            a_send.at[n, slot, p], a_recv.at[n, slot, p], (dp, p),
        )

    def send_all(n, slot):
        def one(i, _):
            send_copy(n, slot, peer(i)).start()
            return 0

        lax.fori_loop(1, GROUP, one, 0)

    for n in range(3):
        send_all(n, 0)

    def z_copy(n):
        at = block_at(orders[(0, 1, 2)[n]], y)
        return remote(wb.at[at], wb.at[at], z_send.at[n], z_recv.at[n], (near, twin, near)[n])

    def z_arrival(n):
        at = block_at(orders[n + 1], y)
        return remote(wb.at[at], wb.at[at], z_send.at[n], z_recv.at[n], (near, twin, near)[n])

    def y_copy(way, at):
        view = wb.at[at, :, y_cols]
        return remote(view, view, y_send.at[way, at], y_recv.at[at], ring[way])

    def b_copy(at):
        view = wb.at[at, :, b_cols]
        return remote(view, view, b_send.at[at], b_recv.at[at], near)

    def b_arrival(at):
        view = wb.at[at, :, b_cols_in]
        return remote(view, view, b_send.at[at], b_recv.at[at], near)

    def y_first(j):
        at = block_at(orders[j], y)
        for way in range(2):
            y_copy(way, at).start()

    def y_round(e):
        for way in range(2):
            j, t = ARRIVALS[way][e]
            step = (NY - 1 - t) if way == 0 else t + 1
            at = block_at(orders[j], (y + step) % NY)
            y_copy(way, at).wait_recv()
            if t + 1 < STEPS[way][j]:
                y_copy(way, at).start()
            b_copy(at).start()

    w_local.wait()
    w_sib.wait_recv()
    z_copy(0).start()
    y_first(0)
    for n in range(3):
        send_all(n, 1)
    r_sib = remote(res_in.at[0, :, theirs], rb.at[core], s_send.at[1], s_recv.at[1], sib)
    r_sib.start()
    g_local.wait()
    g_sib = remote(gs.at[:, theirs], gb.at[core], s_send.at[2], s_recv.at[2], sib)
    g_sib.start()

    def z_done(n):
        z_arrival(n).wait_recv()
        if n < 2:
            z_copy(n + 1).start()
        y_first(n + 1)

    def o_copy(slot, p):
        return remote(
            stage.at[slot, p], ob.at[slot, core, :, pl.ds(pl.multiple_of(me * HEAD_DIM, HEAD_DIM), HEAD_DIM)],
            o_send.at[slot, p], o_recv.at[slot, me], (dp, p),
        )

    def o_arrival(slot, p):
        return remote(
            stage.at[slot, p], ob.at[slot, core, :, pl.ds(pl.multiple_of(p * HEAD_DIM, HEAD_DIM), HEAD_DIM)],
            o_send.at[slot, p], o_recv.at[slot, p], (dp, p),
        )

    def o_own(slot):
        return pltpu.make_async_copy(
            stage.at[slot, me],
            ob.at[slot, core, :, pl.ds(pl.multiple_of(me * HEAD_DIM, HEAD_DIM), HEAD_DIM)],
            o_loc.at[slot],
        )

    factor = math.log2(math.e) / math.sqrt(HEAD_DIM)
    per_tile = GROUP // NTILES
    tile = per_tile * tok

    def attend(slot, p):
        head = me * SLOTS + slot
        q_tile = p // per_tile
        count = counts[head, q_tile]
        listed = [tiles[head, q_tile, n] for n in range(NTILES)]
        queries = qb[slot, p]
        scores, peaks, seen = [], [], []
        for t in range(NTILES):
            keys = kb[slot, t * per_tile : (t + 1) * per_tile].reshape(tile, HEAD_DIM)
            s = lax.dot_general(
                queries, keys, (((1,), (1,)), ((), ())), preferred_element_type=jnp.float32
            )
            scores.append(s)
            peaks.append(jnp.max(s, axis=1, keepdims=True))
            hits = jnp.int32(0)
            for n in range(NTILES):
                hits = hits + jnp.where((listed[n] == t) & (n < count), 1, 0)
            seen.append(hits > 0)
        peak = None
        for t in range(NTILES):
            here = jnp.where(seen[t], peaks[t], -jnp.inf)
            peak = here if peak is None else jnp.maximum(peak, here)
        total, mixed = None, None
        for t in range(NTILES):
            shift = jnp.where(seen[t], peak * factor, jnp.inf)
            weights = jnp.exp2(scores[t] * factor - shift)
            values = vb[slot, t * per_tile : (t + 1) * per_tile].reshape(tile, HEAD_DIM)
            part = jnp.dot(weights.astype(jnp.bfloat16), values, preferred_element_type=jnp.float32)
            row = jnp.sum(weights, axis=1, keepdims=True)
            total = row if total is None else total + row
            mixed = part if mixed is None else mixed + part
        stage[slot, p] = (mixed / total).astype(jnp.bfloat16)

    def head_pass(slot, between):
        own_copy(0, slot).wait()
        own_copy(2, slot).wait()
        own_copy(1, slot).wait()

        def landed(i, _):
            arrival(0, slot, peer(i)).wait_recv()
            arrival(2, slot, peer(i)).wait_recv()
            return 0

        lax.fori_loop(1, GROUP, landed, 0)

        def one(i, _):
            p = peer(i)

            @pl.when(i > 0)
            def _():
                arrival(1, slot, p).wait_recv()

            attend(slot, p)

            @pl.when(i > 0)
            def _():
                o_copy(slot, p).start()

            for at, work in between.items():

                @pl.when(i == at)
                def _(work=work):
                    work()

            return 0

        lax.fori_loop(0, GROUP, one, 0)
        o_own(slot).start()

    def o_landed(slot):
        def one(i, _):
            o_arrival(slot, peer(i)).wait_recv()
            return 0

        lax.fori_loop(1, GROUP, one, 0)
        o_own(slot).wait()

    def forward(slot):
        view = ob.at[slot, core]
        return remote(view, view, f_send.at[slot], f_recv.at[slot], sib)

    def forwarded(slot):
        view = ob.at[slot, other]
        return remote(view, view, f_send.at[slot], f_recv.at[slot], sib)

    z_done(0)
    y_round(0)
    y_round(1)
    y_round(2)
    z_done(1)
    y_round(3)
    y_round(4)
    head_pass(0, {2: lambda: y_round(5), 5: lambda: (z_done(2), y_round(6))})
    y_round(7)
    y_round(8)
    head_pass(1, {2: lambda: y_round(9), 5: lambda: y_round(10)})
    o_landed(0)
    forward(0).start()
    y_round(11)
    o_landed(1)
    forward(1).start()
    y_round(12)
    y_round(13)
    r_local.wait()
    r_sib.wait_recv()
    g_sib.wait_recv()

    def blocks_done(u, _):
        at = block_at(u // (NY - 1), (y + 1 + u % (NY - 1)) % NY)
        b_arrival(at).wait_recv()
        return 0

    lax.fori_loop(0, NZ_HI * (NY - 1), blocks_done, 0)
    forwarded(0).wait_recv()
    forwarded(1).wait_recv()

    wide = outv.shape[3]
    parts = outv.shape[0]

    def out_cols(n):
        return pl.ds(pl.multiple_of(core * half + n * wide, 128), wide)

    def out_own(n):
        return pltpu.make_async_copy(outv.at[n, core], out.at[0, :, out_cols(n)], p_loc.at[n])

    def out_sib(n):
        return remote(outv.at[n, other], out.at[0, :, out_cols(n)], p_send.at[n], p_recv.at[n], sib)

    def out_sib_in(n):
        cols = pl.ds(pl.multiple_of(other * half + n * wide, 128), wide)
        return remote(outv.at[n, other], out.at[0, :, cols], p_send.at[n], p_recv.at[n], sib)

    per_slot = wb.shape[0] // SLOTS
    depth = per_slot * wb.shape[1]

    def project(n, _):
        cols = pl.ds(pl.multiple_of(n * wide, 128), wide)
        acc = None
        for slot in range(SLOTS):
            part = jnp.dot(
                ob[slot].reshape(NCORE * tok, depth),
                wb[slot * per_slot : (slot + 1) * per_slot, :, cols].reshape(depth, wide),
                preferred_element_type=jnp.float32,
            )
            acc = part if acc is None else acc + part
        for clip in range(NCORE):
            rows = acc[clip * tok : (clip + 1) * tok]
            mixed = rb[clip, :, cols].astype(jnp.float32) + gb[clip, 0:1, cols] * rows
            outv[n, clip] = mixed.astype(jnp.bfloat16)
        out_own(n).start()
        out_sib(n).start()
        return 0

    lax.fori_loop(0, parts, project, 0)

    for slot in range(SLOTS):
        for n in range(3):

            def sent(i, _, n=n, slot=slot):
                send_copy(n, slot, peer(i)).wait_send()
                return 0

            lax.fori_loop(1, GROUP, sent, 0)

        def o_sent(i, _, slot=slot):
            o_copy(slot, peer(i)).wait_send()
            return 0

        lax.fori_loop(1, GROUP, o_sent, 0)
        forward(slot).wait_send()
    for n in range(3):
        z_copy(n).wait_send()
    for way in range(2):
        for j in range(NZ_HI):
            for t in range(STEPS[way][j]):
                step = (NY - t) if way == 0 else t
                y_copy(way, block_at(orders[j], (y + step) % NY)).wait_send()

    def b_sent(u, _):
        at = block_at(u // (NY - 1), (y + 1 + u % (NY - 1)) % NY)
        b_copy(at).wait_send()
        return 0

    lax.fori_loop(0, NZ_HI * (NY - 1), b_sent, 0)
    w_sib.wait_send()
    r_sib.wait_send()
    g_sib.wait_send()

    def out_done(n, _):
        out_own(n).wait()
        out_sib(n).wait_send()
        out_sib_in(n).wait_recv()
        return 0

    lax.fori_loop(0, parts, out_done, 0)


def on_device(
    query_rows, key_rows, value_rows, key_tiles, tile_counts, out_weight, gate_scale, residual
):
    tok, feats = query_rows.shape[1:]
    w_rows, width = out_weight.shape
    half = width // NCORE
    parts = 6
    bf16, f32 = jnp.bfloat16, jnp.float32
    dma = pltpu.SemaphoreType.DMA
    blocks = NZ_HI * NY
    hbm = pl.BlockSpec(memory_space=pl.ANY)
    smem = pl.BlockSpec(memory_space=pltpu.SMEM)
    vmem = pl.BlockSpec(memory_space=pltpu.VMEM)
    return pl.pallas_call(
        kernel,
        out_shape=jax.ShapeDtypeStruct(residual.shape, residual.dtype),
        in_specs=[hbm, hbm, hbm, smem, smem, hbm, vmem, hbm],
        out_specs=hbm,
        scratch_shapes=[
            pltpu.VMEM((SLOTS, GROUP, tok, HEAD_DIM), bf16),
            pltpu.VMEM((SLOTS, GROUP, tok, HEAD_DIM), bf16),
            pltpu.VMEM((SLOTS, GROUP, tok, HEAD_DIM), bf16),
            pltpu.VMEM((SLOTS, GROUP, tok, HEAD_DIM), bf16),
            pltpu.VMEM((SLOTS, NCORE, tok, feats // SLOTS), bf16),
            pltpu.VMEM((blocks, NCORE * w_rows, half), bf16),
            pltpu.VMEM((NCORE, tok, half), bf16),
            pltpu.VMEM((8, width), f32),
            pltpu.VMEM((NCORE, 8, half), f32),
            pltpu.VMEM((parts, NCORE, tok, half // parts), bf16),
            dma((3, SLOTS, GROUP)),
            dma((3, SLOTS, GROUP)),
            dma((3, SLOTS)),
            dma((SLOTS, GROUP)),
            dma((SLOTS, GROUP)),
            dma((SLOTS,)),
            dma((SLOTS,)),
            dma((SLOTS,)),
            dma((2, blocks)),
            dma((blocks,)),
            dma((blocks,)),
            dma((blocks,)),
            dma((3,)),
            dma((3,)),
            dma((3,)),
            dma((3,)),
            dma((3,)),
            dma((parts,)),
            dma((parts,)),
            dma((parts,)),
        ],
        compiler_params=pltpu.CompilerParams(
            collective_id=0, has_side_effects=True, vmem_limit_bytes=56 << 20
        ),
    )(query_rows, key_rows, value_rows, key_tiles, tile_counts, out_weight, gate_scale, residual)


def solution(mesh):
    in_specs = (
        P("dp", "seq", None),
        P("dp", "seq", None),
        P("dp", "seq", None),
        P(),
        P(),
        P("dp", None),
        P("dp", None),
        P("dp", "seq", None),
    )
    return jax.shard_map(
        on_device, mesh=mesh, in_specs=in_specs, out_specs=P("dp", "seq", None), check_vma=False
    )
```

time: 173 us -> 99.4 us (0.57)
  the two profiles are of different devices: /device:TPU:48 before, /device:TPU:1 now
where the time goes in v1:
time: 99.4 us; the launch traced here: 99.1 us
  Pallas kernels  93.9 us (94%)
  local copies, waits for them, and re-layouts  5.11 us (5%)
    pallas_call x1, Pallas kernels, on_device(): pl.pallas_call(kernel, out_shape=jax.ShapeDtypeStruct(residual.shape, res...  93.9 us
    unnamed x3, local copies, waits for them, and re-layouts  5.11 us

profile of v1, /device:TPU:1, one launch (start us, length us, event | category | flops | bytes accessed | tf_op | source)
XLA Modules:
  0.0 99.1 jit_solution(15801819748910200850)
XLA Ops:
  0.0 1.3 %copy.10.counts = s32[16,4]{1,0:T(8,128)} copy(s32[16,4]{0,1:T(4,128)} %param.12) | data formatting | bytes 512 | tf_op args[4]
  1.3 1.4 %copy.9.tiles = s32[16,4,4]{2,1,0:T(4,128)} copy(s32[16,4,4]{0,2,1:T(4,128)} %param.11) | data formatting | bytes 2048 | tf_op args[3]
  2.8 93.9 %shard_map.82 = bf16[1,192,3072]{2,1,0:T(8,128)(2,1)} custom-call(bf16[1,192,2048]{2,1,0:T(8,128)(2,1)} %q_in.1, bf16[1,192,2048]{2,1,0:T(8,128)(2,1)} %k_in.1, bf16[1,192,2048]{2,1,0:T(8,128)(2,1)} %v_in.1, s32[16,4,4]{2,1,0:T(4,128)} %copy.9.tiles, s32[16,4]{1,0:T(8,128)} %copy.10.counts, bf16[32,3072]{1,0:T(8,128)(2,1)} %w_in.1, bf16[1,3072]{1,0:T(2,128)(2,1)} %gate_in.1, ...), custom_call_target="tpu_custom_call" | custom-call | tf_op jit(solution)/shard_map/pallas_call | solution.py:422
  96.7 2.4 %copy.12 = bf16[1,192,3072]{2,1,0:T(8,128)(2,1)} copy(bf16[1,192,3072]{2,1,0:T(8,128)(2,1)} %shard_map.82) | data formatting | bytes 2359296

commit v2 on v1

v2 whole, which is shorter than its diff:
```python
import functools
import math

import jax
import jax.numpy as jnp
from jax import lax
from jax.experimental import pallas as pl
from jax.experimental.pallas import tpu as pltpu
from jax.sharding import PartitionSpec as P

MESH = pl.DeviceIdType.MESH

HEAD_DIM = 128
NX, NZ_LO = 4, 2
NY, NZ_HI, NCORE = 8, 4, 2
GROUP = NX * NZ_LO
SLOTS = 2
NTILES = 4
SHARED = 384
STEPS = ((4, 3, 4, 3), (3, 4, 3, 4))
ARRIVALS = (
    ((0, 0), (1, 0), (0, 1), (2, 0), (1, 1), (0, 2), (3, 0), (2, 1), (1, 2), (3, 1), (0, 3), (2, 2), (3, 2), (2, 3)),
    ((0, 0), (1, 0), (0, 1), (2, 0), (1, 1), (0, 2), (3, 0), (1, 2), (3, 1), (2, 1), (3, 2), (1, 3), (2, 2), (3, 3)),
)


def kernel(
    q_in, k_in, v_in, tiles, counts, w_in, gate_in, res_in, out,
    qb, kb, vb, stage, ob, wb, rb, gs, gb, sums, outv,
    a_send, a_recv, a_loc, o_send, o_recv, o_loc, f_send, f_recv, y_send, y_recv, x_send, x_recv,
    b_send, b_recv, z_send, z_recv, s_send, s_recv, s_loc, p_send, p_recv, p_loc,
):
    dp, me = lax.axis_index("dp"), lax.axis_index("seq")
    z_hi, y, core = dp // (NY * NCORE), (dp // NCORE) % NY, dp % NCORE
    z_lo, x = me // NX, me % NX
    way_z = 2 * z_lo - 1
    tok = q_in.shape[1]
    half = w_in.shape[1] // 2
    other = 1 - core

    sib = (dp + 1 - 2 * core, me)
    ring = tuple(
        (z_hi * NY * NCORE + ((y + d) % NY) * NCORE + core, me) for d in (1, NY - 1)
    )
    near = (((z_hi + way_z + NZ_HI) % NZ_HI) * NY * NCORE + y * NCORE + core, (1 - z_lo) * NX + x)
    twin = (dp, (1 - z_lo) * NX + x)
    beside = tuple((dp, z_lo * NX + (x + d) % NX) for d in (1, NX - 1))
    kept, skipped = 1 - x % 2, x % 2

    def peer(i):
        return ((z_lo + i // NX) % NZ_LO) * NX + (x + i) % NX

    def block_at(zh, yy):
        return ((yy // 2) % 2) * 16 + (zh * 2 + yy // 4) * 2 + yy % 2

    def shard_at(zh, yy, part):
        return block_at(zh, yy) * NCORE + (core + part) % NCORE

    def remote(src, dst, send, recv, to):
        return pltpu.make_async_remote_copy(
            src_ref=src, dst_ref=dst, send_sem=send, recv_sem=recv, device_id=to, device_id_type=MESH
        )

    def all_sent(view, sem):
        remote(view, view, sem, sem, sib).wait_send()

    def all_landed(view, sem):
        remote(view, view, sem, sem, sib).wait_recv()

    def head_cols(p, slot):
        return pl.ds(pl.multiple_of((p * SLOTS + slot) * HEAD_DIM, HEAD_DIM), HEAD_DIM)

    mine = pl.ds(pl.multiple_of(core * half, 128), half)
    theirs = pl.ds(pl.multiple_of(other * half, 128), half)
    orders = tuple(
        (z_hi + NZ_HI + off) % NZ_HI for off in (0, way_z, -way_z, 2)
    )
    y_cols = pl.ds(pl.multiple_of(z_lo * SHARED, 128), half - SHARED)
    b_cols = pl.ds(pl.multiple_of(z_lo * (half - SHARED), 128), SHARED)
    b_cols_in = pl.ds(pl.multiple_of((1 - z_lo) * (half - SHARED), 128), SHARED)
    own_shard = shard_at(z_hi, y, 0)

    w_local = pltpu.make_async_copy(
        w_in.at[:, mine], wb.at[own_shard], s_loc.at[0]
    )
    w_local.start()
    tensors = ((k_in, kb), (q_in, qb), (v_in, vb))

    def own_copy(n, slot):
        src, dst = tensors[n]
        return pltpu.make_async_copy(src.at[0, :, head_cols(me, slot)], dst.at[slot, me], a_loc.at[slot])

    for slot in range(SLOTS):
        for n in range(3):
            own_copy(n, slot).start()
    r_local = pltpu.make_async_copy(res_in.at[0, :, mine], rb.at[core], s_loc.at[1])
    r_local.start()
    gs[...] = jnp.broadcast_to(gate_in[...].astype(jnp.float32), gs.shape)
    g_local = pltpu.make_async_copy(gs.at[:, mine], gb.at[core], s_loc.at[2])
    g_local.start()

    barrier = pltpu.get_barrier_semaphore()
    for to in (sib, *ring, near):
        pl.semaphore_signal(barrier, inc=1, device_id=to, device_id_type=MESH)

    def greet(i, _):
        pl.semaphore_signal(barrier, inc=1, device_id=(dp, peer(i)), device_id_type=MESH)
        return 0

    lax.fori_loop(1, GROUP, greet, 0)
    pl.semaphore_wait(barrier, GROUP + 3)

    w_sib = remote(
        w_in.at[:, theirs],
        wb.at[own_shard],
        s_send.at[0], s_recv.at[0], sib,
    )
    w_sib.start()

    def send_all(slot, lo, hi):
        for n in range(3):
            src, dst = tensors[n]

            def one(i, _, n=n, src=src, dst=dst):
                p = peer(i)
                if n == 1:
                    done = a_recv.at[slot, 1 + i // NX]
                else:
                    done = a_recv.at[slot, 0]
                remote(
                    src.at[0, :, head_cols(p, slot)], dst.at[slot, me], a_send.at[n], done, (dp, p)
                ).start()
                return 0

            lax.fori_loop(lo, hi, one, 0)

    def z_copy(n, part):
        view = wb.at[shard_at(orders[n], y, part)]
        return remote(view, view, z_send, z_recv.at[n, part], (near, twin, near)[n])

    def z_arrival(n, part):
        view = wb.at[shard_at(orders[n + 1], y, part)]
        return remote(view, view, z_send, z_recv.at[n, part], (near, twin, near)[n])

    def y_copy(way, at):
        view = wb.at[at, :, y_cols]
        return remote(view, view, y_send, y_recv.at[at], ring[way])

    def x_copy(way, t, at):
        view = wb.at[at, :, y_cols]
        return remote(view, view, x_send, x_recv.at[way, t], beside[way])

    def b_copy(j, at):
        view = wb.at[at, :, b_cols]
        return remote(view, view, b_send, b_recv.at[j // 2], near)

    def y_first(j, part):
        at = shard_at(orders[j], y, part)
        for way in range(2):
            y_copy(way, at).start()

    def row_of(way, t):
        return (y + ((NY - 1 - t) if way == 0 else t + 1)) % NY

    def y_round(e):
        for part in range(NCORE):
            for way in range(2):
                j, t = ARRIVALS[way][e]
                if j == 3 and part:
                    continue
                at = shard_at(orders[j], row_of(way, t), kept if j == 3 else part)
                y_copy(way, at).wait_recv()
                if t + 1 < STEPS[way][j]:
                    y_copy(way, at).start()
                if j == 3:
                    x_copy(way, t, at).start()
                b_copy(j, at).start()

    def x_done(way, t):
        at = shard_at(orders[3], row_of(way, t), skipped)
        x_copy(way, t, at).wait_recv()
        b_copy(3, at).start()

    def z_done(n):
        for part in range(NCORE):
            z_arrival(n, part).wait_recv()
            if n < 2:
                z_copy(n + 1, part).start()
                y_first(n + 1, part)
        if n == 2:
            y_first(3, kept)

    w_local.wait()
    z_copy(0, 0).start()
    y_first(0, 0)
    send_all(0, 1, NX)
    w_sib.wait_recv()
    z_copy(0, 1).start()
    y_first(0, 1)
    r_sib = remote(res_in.at[0, :, theirs], rb.at[core], s_send.at[1], s_recv.at[1], sib)
    r_sib.start()
    g_local.wait()
    g_sib = remote(gs.at[:, theirs], gb.at[core], s_send.at[2], s_recv.at[2], sib)
    g_sib.start()

    def o_copy(slot, p):
        return remote(
            stage.at[slot, p], ob.at[slot, core, :, pl.ds(pl.multiple_of(me * HEAD_DIM, HEAD_DIM), HEAD_DIM)],
            o_send, o_recv.at[slot], (dp, p),
        )

    def o_own(slot):
        return pltpu.make_async_copy(
            stage.at[slot, me],
            ob.at[slot, core, :, pl.ds(pl.multiple_of(me * HEAD_DIM, HEAD_DIM), HEAD_DIM)],
            o_loc.at[slot],
        )

    factor = math.log2(math.e) / math.sqrt(HEAD_DIM)
    per_tile = GROUP // NTILES
    tile = per_tile * tok

    def attend(slot, p):
        head = me * SLOTS + slot
        q_tile = p // per_tile
        count = counts[q_tile, head]
        listed = [tiles[q_tile, n, head] for n in range(NTILES)]
        queries = qb[slot, p]
        scores, peaks, seen = [], [], []
        for t in range(NTILES):
            keys = kb[slot, t * per_tile : (t + 1) * per_tile].reshape(tile, HEAD_DIM)
            s = lax.dot_general(
                queries, keys, (((1,), (1,)), ((), ())), preferred_element_type=jnp.float32
            )
            scores.append(s)
            peaks.append(jnp.max(s, axis=1, keepdims=True))
            hits = jnp.int32(0)
            for n in range(NTILES):
                hits = hits + jnp.where((listed[n] == t) & (n < count), 1, 0)
            seen.append(hits > 0)
        peak = None
        for t in range(NTILES):
            here = jnp.where(seen[t], peaks[t], -jnp.inf)
            peak = here if peak is None else jnp.maximum(peak, here)
        total, mixed = None, None
        for t in range(NTILES):
            shift = jnp.where(seen[t], peak * factor, jnp.inf)
            weights = jnp.exp2(scores[t] * factor - shift)
            values = vb[slot, t * per_tile : (t + 1) * per_tile].reshape(tile, HEAD_DIM)
            part = jnp.dot(weights.astype(jnp.bfloat16), values, preferred_element_type=jnp.float32)
            row = jnp.sum(weights, axis=1, keepdims=True)
            total = row if total is None else total + row
            mixed = part if mixed is None else mixed + part
        stage[slot, p] = (mixed / total).astype(jnp.bfloat16)

    def head_pass(slot, between):
        here = qb.at[0, 0:3]
        pltpu.make_async_copy(here, here, a_loc.at[slot]).wait()
        all_landed(kb.at[0:2, 0 : GROUP - 1], a_recv.at[slot, 0])

        def one(i, _):
            p = peer(i)

            @pl.when(i == 1)
            def _():
                all_landed(qb.at[slot, 0 : NX - 1], a_recv.at[slot, 1])

            @pl.when(i == NX)
            def _():
                all_landed(qb.at[slot, 0:NX], a_recv.at[slot, 2])

            attend(slot, p)

            @pl.when(i > 0)
            def _():
                o_copy(slot, p).start()

            for at, work in between.items():

                @pl.when(i == at)
                def _(work=work):
                    work()

            return 0

        lax.fori_loop(0, GROUP, one, 0)
        o_own(slot).start()

    def o_landed(slot):
        all_landed(stage.at[slot, 0 : GROUP - 1], o_recv.at[slot])
        o_own(slot).wait()

    def forward(slot):
        view = ob.at[slot, core]
        return remote(view, view, f_send, f_recv, sib)

    z_done(0)
    send_all(0, NX, GROUP)
    send_all(1, 1, GROUP)
    y_round(0)
    y_round(1)
    z_done(1)
    y_round(2)
    y_round(3)
    z_done(2)
    y_round(4)
    head_pass(0, {2: lambda: y_round(5), 5: lambda: y_round(6)})
    y_round(7)
    y_round(8)
    x_done(0, 0)
    x_done(1, 0)
    y_round(9)
    head_pass(1, {2: lambda: y_round(10), 5: lambda: y_round(11)})
    x_done(0, 1)
    x_done(1, 1)
    o_landed(0)
    forward(0).start()
    y_round(12)
    x_done(1, 2)
    o_landed(1)
    forward(1).start()
    y_round(13)
    x_done(0, 2)
    x_done(1, 3)
    r_local.wait()
    r_sib.wait_recv()
    g_sib.wait_recv()
    all_landed(ob.at[:, 0], f_recv)

    wide = outv.shape[3]
    parts = outv.shape[0]

    def out_cols(n):
        return pl.ds(pl.multiple_of(core * half + n * wide, 128), wide)

    def out_own(n):
        return pltpu.make_async_copy(outv.at[n, core], out.at[0, :, out_cols(n)], p_loc)

    def out_sib(n):
        return remote(outv.at[n, other], out.at[0, :, out_cols(n)], p_send, p_recv, sib)

    per_slot = wb.shape[0] // SLOTS
    per_zh = per_slot // NZ_HI
    depth = per_zh * wb.shape[1]

    def products(pair, cols):
        acc = None
        for j in pair:
            zh = orders[j]
            feats = pl.ds(pl.multiple_of(zh * depth, 128), depth)
            for slot in range(SLOTS):
                part = jnp.dot(
                    ob[slot, :, :, feats].reshape(NCORE * tok, depth),
                    wb[pl.ds(slot * per_slot + zh * per_zh, per_zh), :, cols].reshape(depth, wide),
                    preferred_element_type=jnp.float32,
                )
                acc = part if acc is None else acc + part
        return acc

    def early(n, _):
        sums[n] = products((0, 1), pl.ds(pl.multiple_of(n * wide, 128), wide))
        return 0

    def late(n, _):
        cols = pl.ds(pl.multiple_of(n * wide, 128), wide)
        acc = sums[n] + products((2, 3), cols)
        for clip in range(NCORE):
            rows = acc[clip * tok : (clip + 1) * tok]
            mixed = rb[clip, :, cols].astype(jnp.float32) + gb[clip, 0:1, cols] * rows
            outv[n, clip] = mixed.astype(jnp.bfloat16)
        out_own(n).start()
        out_sib(n).start()
        return 0

    half_far = NCORE * NZ_HI * (NY - 1) // 2
    all_landed(wb.at[0:half_far, :, 0:SHARED], b_recv.at[0])
    lax.fori_loop(0, parts, early, 0)
    all_landed(wb.at[0:half_far, :, 0:SHARED], b_recv.at[1])
    lax.fori_loop(0, parts, late, 0)

    for n in range(3):
        all_sent(kb.at[0:2, 0 : GROUP - 1], a_send.at[n])
    all_sent(stage.at[0:2, 0 : GROUP - 1], o_send)
    all_sent(ob.at[:, 0], f_send)
    all_sent(wb.at[0 : 3 * NCORE], z_send)
    all_sent(wb.at[0 : (NCORE * NZ_HI - 1) * (NY - 1), :, 0 : half - SHARED], y_send)
    all_sent(wb.at[0 : NY - 1, :, 0 : half - SHARED], x_send)
    all_sent(wb.at[0 : 2 * half_far, :, 0:SHARED], b_send)
    w_sib.wait_send()
    r_sib.wait_send()
    g_sib.wait_send()
    pltpu.make_async_copy(outv.at[:, 0], outv.at[:, 0], p_loc).wait()
    all_sent(outv.at[:, 0], p_send)
    all_landed(outv.at[:, 0], p_recv)


def on_device(
    query_rows, key_rows, value_rows, key_tiles, tile_counts, out_weight, gate_scale, residual
):
    tok, feats = query_rows.shape[1:]
    w_rows, width = out_weight.shape
    half = width // NCORE
    parts = 6
    bf16, f32 = jnp.bfloat16, jnp.float32
    dma = pltpu.SemaphoreType.DMA
    shards = NZ_HI * NY * NCORE
    hbm = pl.BlockSpec(memory_space=pltpu.HBM)
    smem = pl.BlockSpec(memory_space=pltpu.SMEM)
    vmem = pl.BlockSpec(memory_space=pltpu.VMEM)
    return pl.pallas_call(
        kernel,
        out_shape=jax.ShapeDtypeStruct(residual.shape, residual.dtype),
        in_specs=[hbm, hbm, hbm, smem, smem, hbm, vmem, hbm],
        out_specs=pl.BlockSpec(memory_space=pl.ANY),
        scratch_shapes=[
            pltpu.VMEM((SLOTS, GROUP, tok, HEAD_DIM), bf16),
            pltpu.VMEM((SLOTS, GROUP, tok, HEAD_DIM), bf16),
            pltpu.VMEM((SLOTS, GROUP, tok, HEAD_DIM), bf16),
            pltpu.VMEM((SLOTS, GROUP, tok, HEAD_DIM), bf16),
            pltpu.VMEM((SLOTS, NCORE, tok, feats // SLOTS), bf16),
            pltpu.VMEM((shards, w_rows, half), bf16),
            pltpu.VMEM((NCORE, tok, half), bf16),
            pltpu.VMEM((8, width), f32),
            pltpu.VMEM((NCORE, 8, half), f32),
            pltpu.VMEM((parts, NCORE * tok, half // parts), f32),
            pltpu.VMEM((parts, NCORE, tok, half // parts), bf16),
            dma((3,)),
            dma((SLOTS, 3)),
            dma((SLOTS,)),
            dma,
            dma((SLOTS,)),
            dma((SLOTS,)),
            dma,
            dma,
            dma,
            dma((shards,)),
            dma,
            dma((2, 4)),
            dma,
            dma((2,)),
            dma,
            dma((3, NCORE)),
            dma((3,)),
            dma((3,)),
            dma((3,)),
            dma,
            dma,
            dma,
        ],
        compiler_params=pltpu.CompilerParams(
            collective_id=0, has_side_effects=True, vmem_limit_bytes=56 << 20
        ),
    )(
        query_rows, key_rows, value_rows, jnp.transpose(key_tiles, (1, 2, 0)), tile_counts.T,
        out_weight, gate_scale, residual,
    )


def solution(mesh):
    in_specs = (
        P("dp", "seq", None),
        P("dp", "seq", None),
        P("dp", "seq", None),
        P(),
        P(),
        P("dp", None),
        P("dp", None),
        P("dp", "seq", None),
    )
    return jax.shard_map(
        on_device, mesh=mesh, in_specs=in_specs, out_specs=P("dp", "seq", None), check_vma=False
    )
```

time: 99.4 us -> 75.3 us (0.76)
  Pallas kernels: 93.9 us -> 72.7 us
  local copies, waits for them, and re-layouts: 5.11 us -> 2.36 us
    pallas_call x1, Pallas kernels: 93.9 us -> 72.7 us  [on_device(): pl.pallas_call(kernel, out_shape=jax.ShapeDtypeStruct(residual.shape, res...]
    unnamed x3 -> x1, local copies, waits for them, and re-layouts: 5.11 us -> 2.36 us
where the time goes in v2:
time: 75.3 us; the launch traced here: 75.1 us
  Pallas kernels  72.7 us (97%)
  local copies, waits for them, and re-layouts  2.36 us (3%)
    pallas_call x1, Pallas kernels, on_device(): pl.pallas_call(kernel, out_shape=jax.ShapeDtypeStruct(residual.shape, res...  72.7 us
    unnamed x1, local copies, waits for them, and re-layouts  2.36 us

profile of v2, /device:TPU:1, one launch (start us, length us, event | category | flops | bytes accessed | tf_op | source)
XLA Modules:
  0.0 75.1 jit_solution(15218982304468711572)
XLA Ops:
  0.0 72.7 %shard_map.82 = bf16[1,192,3072]{2,1,0:T(8,128)(2,1)} custom-call(bf16[1,192,2048]{2,1,0:T(8,128)(2,1)} %q_in.1, bf16[1,192,2048]{2,1,0:T(8,128)(2,1)} %k_in.1, bf16[1,192,2048]{2,1,0:T(8,128)(2,1)} %v_in.1, s32[4,4,16]{2,1,0:T(4,128)} %bitcast.2, s32[4,16]{1,0:T(4,128)} %bitcast.3, bf16[32,3072]{1,0:T(8,128)(2,1)} %w_in.1, bf16[1,3072]{1,0:T(2,128)(2,1)} %gate_in.1, ...), custom_call_target="tpu_custom_call" | custom-call | tf_op jit(solution)/shard_map/pallas_call | solution.py:410
  72.7 2.4 %copy.10 = bf16[1,192,3072]{2,1,0:T(8,128)(2,1)} copy(bf16[1,192,3072]{2,1,0:T(8,128)(2,1)} %shard_map.82) | data formatting | bytes 2359296

commit v3 on v2

--- a/solution.py
+++ b/solution.py
@@ -18,9 +18,24 @@
 NTILES = 4
 SHARED = 384
 STEPS = ((4, 3, 4, 3), (3, 4, 3, 4))
-ARRIVALS = (
-    ((0, 0), (1, 0), (0, 1), (2, 0), (1, 1), (0, 2), (3, 0), (2, 1), (1, 2), (3, 1), (0, 3), (2, 2), (3, 2), (2, 3)),
-    ((0, 0), (1, 0), (0, 1), (2, 0), (1, 1), (0, 2), (3, 0), (1, 2), (3, 1), (2, 1), (3, 2), (1, 3), (2, 2), (3, 3)),
+BESIDE = 1
+ORDER = (
+    (("y", 0, 0, 0, 0), ("y", 1, 0, 0, 0), ("z", 0, 0), ("y", 0, 0, 1, 0), ("y", 1, 0, 1, 0), ("z", 0, 1),
+     ("y", 0, 0, 0, 1), ("y", 1, 0, 0, 1), ("z", 1, 0), ("y", 0, 1, 0, 0), ("y", 1, 1, 0, 0), ("z", 1, 1),
+     ("y", 0, 0, 1, 1), ("y", 1, 0, 1, 1), ("y", 0, 0, 0, 2), ("y", 1, 0, 0, 2), ("z", 2, 0),
+     ("y", 0, 2, 0, 0), ("y", 1, 2, 0, 0), ("y", 0, 1, 0, 1), ("y", 1, 1, 0, 1), ("z", 2, 1),
+     ("y", 0, 2, 1, 0), ("y", 1, 2, 1, 0), ("y", 0, 0, 1, 2), ("y", 1, 0, 1, 2),),
+    (("y", 0, 0, 0, 3), ("y", 1, 3, 0, 0),),
+    (("y", 0, 3, 0, 0), ("y", 1, 2, 0, 1),),
+    (("y", 0, 2, 0, 1), ("y", 1, 1, 0, 2), ("y", 0, 1, 0, 2), ("y", 1, 3, 1, 0),),
+    (("y", 0, 3, 1, 0), ("y", 1, 2, 1, 1), ("y", 0, 2, 1, 1), ("y", 1, 3, 0, 1), ("y", 0, 0, 1, 3),
+     ("y", 1, 2, 0, 2), ("x", 0, 0), ("x", 1, 0), ("y", 0, 3, 0, 1), ("y", 1, 1, 0, 3), ("x", 0, 1),
+     ("x", 1, 1),),
+    (("y", 0, 2, 0, 2), ("y", 1, 3, 1, 1),),
+    (("y", 0, 3, 1, 1), ("y", 1, 2, 1, 2),),
+    (("y", 0, 2, 1, 2), ("y", 1, 3, 0, 2), ("x", 1, 2), ("x", 0, 2), ("y", 0, 3, 0, 2), ("y", 1, 3, 1, 2),),
+    (("x", 1, 3), ("y", 0, 2, 0, 3), ("y", 1, 3, 0, 3), ("y", 0, 3, 1, 2), ("y", 1, 3, 1, 3),
+     ("y", 0, 2, 1, 3),),
 )
 
 
@@ -84,7 +99,7 @@
         w_in.at[:, mine], wb.at[own_shard], s_loc.at[0]
     )
     w_local.start()
-    tensors = ((k_in, kb), (q_in, qb), (v_in, vb))
+    tensors = ((k_in, kb), (v_in, vb), (q_in, qb))
 
     def own_copy(n, slot):
         src, dst = tensors[n]
@@ -123,7 +138,7 @@
 
             def one(i, _, n=n, src=src, dst=dst):
                 p = peer(i)
-                if n == 1:
+                if n == 2:
                     done = a_recv.at[slot, 1 + i // NX]
                 else:
                     done = a_recv.at[slot, 0]
@@ -154,41 +169,50 @@
         view = wb.at[at, :, b_cols]
         return remote(view, view, b_send, b_recv.at[j // 2], near)
 
+    def shard_of(j, yy, part):
+        return shard_at(orders[j], yy, kept if j == BESIDE else part)
+
     def y_first(j, part):
-        at = shard_at(orders[j], y, part)
+        if j == BESIDE and part:
+            return
+        at = shard_of(j, y, part)
         for way in range(2):
             y_copy(way, at).start()
 
     def row_of(way, t):
         return (y + ((NY - 1 - t) if way == 0 else t + 1)) % NY
 
-    def y_round(e):
-        for part in range(NCORE):
-            for way in range(2):
-                j, t = ARRIVALS[way][e]
-                if j == 3 and part:
-                    continue
-                at = shard_at(orders[j], row_of(way, t), kept if j == 3 else part)
-                y_copy(way, at).wait_recv()
-                if t + 1 < STEPS[way][j]:
-                    y_copy(way, at).start()
-                if j == 3:
-                    x_copy(way, t, at).start()
-                b_copy(j, at).start()
+    def y_done(way, j, part, t):
+        at = shard_of(j, row_of(way, t), part)
+        y_copy(way, at).wait_recv()
+        if t + 1 < STEPS[way][j]:
+            y_copy(way, at).start()
+        if j == BESIDE:
+            x_copy(way, t, at).start()
+        b_copy(j, at).start()
 
     def x_done(way, t):
-        at = shard_at(orders[3], row_of(way, t), skipped)
+        at = shard_at(orders[BESIDE], row_of(way, t), skipped)
         x_copy(way, t, at).wait_recv()
-        b_copy(3, at).start()
-
-    def z_done(n):
-        for part in range(NCORE):
-            z_arrival(n, part).wait_recv()
-            if n < 2:
-                z_copy(n + 1, part).start()
-                y_first(n + 1, part)
-        if n == 2:
-            y_first(3, kept)
+        b_copy(BESIDE, at).start()
+
+    def z_done(n, part):
+        z_arrival(n, part).wait_recv()
+        if n < 2:
+            z_copy(n + 1, part).start()
+        if n + 1 != BESIDE:
+            y_first(n + 1, part)
+        elif part:
+            y_first(n + 1, 0)
+        if n == 0 and part:
+            send_all(0, NX, GROUP)
+            send_all(1, 1, GROUP)
+
+    steps = {"z": z_done, "y": y_done, "x": x_done}
+
+    def take(group):
+        for name, *where in ORDER[group]:
+            steps[name](*where)
 
     w_local.wait()
     z_copy(0, 0).start()
@@ -220,12 +244,12 @@
     per_tile = GROUP // NTILES
     tile = per_tile * tok
 
-    def attend(slot, p):
+    def attend(slot, q_tile):
         head = me * SLOTS + slot
-        q_tile = p // per_tile
         count = counts[q_tile, head]
         listed = [tiles[q_tile, n, head] for n in range(NTILES)]
-        queries = qb[slot, p]
+        first = q_tile * per_tile
+        queries = qb[slot, pl.ds(first, per_tile)].reshape(tile, HEAD_DIM)
         scores, peaks, seen = [], [], []
         for t in range(NTILES):
             keys = kb[slot, t * per_tile : (t + 1) * per_tile].reshape(tile, HEAD_DIM)
@@ -251,40 +275,44 @@
             row = jnp.sum(weights, axis=1, keepdims=True)
             total = row if total is None else total + row
             mixed = part if mixed is None else mixed + part
-        stage[slot, p] = (mixed / total).astype(jnp.bfloat16)
-
-    def head_pass(slot, between):
-        here = qb.at[0, 0:3]
-        pltpu.make_async_copy(here, here, a_loc.at[slot]).wait()
-        all_landed(kb.at[0:2, 0 : GROUP - 1], a_recv.at[slot, 0])
-
-        def one(i, _):
-            p = peer(i)
-
-            @pl.when(i == 1)
-            def _():
-                all_landed(qb.at[slot, 0 : NX - 1], a_recv.at[slot, 1])
-
-            @pl.when(i == NX)
-            def _():
-                all_landed(qb.at[slot, 0:NX], a_recv.at[slot, 2])
-
-            attend(slot, p)
-
-            @pl.when(i > 0)
-            def _():
+        done = (mixed / total).astype(jnp.bfloat16)
+        stage[slot, pl.ds(first, per_tile)] = done.reshape(per_tile, tok, HEAD_DIM)
+
+    def part_of_heads(g, _):
+        slot, c = g // NTILES, g % NTILES
+
+        @pl.when(c == 0)
+        def _():
+            here = qb.at[0, 0:3]
+            pltpu.make_async_copy(here, here, a_loc.at[slot]).wait()
+            all_landed(kb.at[0:2, 0 : GROUP - 1], a_recv.at[slot, 0])
+            all_landed(qb.at[0, 0 : NX - 1], a_recv.at[slot, 1])
+
+        @pl.when(c == NTILES // 2)
+        def _():
+            all_landed(qb.at[0, 0:NX], a_recv.at[slot, 2])
+
+        q_tile = ((z_lo + c // 2) % NZ_LO) * (NTILES // NZ_LO) + (x // per_tile + c) % (NTILES // NZ_LO)
+        attend(slot, q_tile)
+        for n in range(per_tile):
+            p = q_tile * per_tile + n
+
+            @pl.when(p != me)
+            def _(p=p):
                 o_copy(slot, p).start()
 
-            for at, work in between.items():
-
-                @pl.when(i == at)
-                def _(work=work):
-                    work()
-
-            return 0
-
-        lax.fori_loop(0, GROUP, one, 0)
-        o_own(slot).start()
+        for group in range(SLOTS * NTILES):
+
+            @pl.when(g == group)
+            def _(group=group):
+                if group % NTILES == 0:
+                    o_own(group // NTILES).start()
+                if group == SLOTS * NTILES - 1:
+                    o_landed(0)
+                    forward(0).start()
+                take(group + 1)
+
+        return 0
 
     def o_landed(slot):
         all_landed(stage.at[slot, 0 : GROUP - 1], o_recv.at[slot])
@@ -292,40 +320,13 @@
 
     def forward(slot):
         view = ob.at[slot, core]
-        return remote(view, view, f_send, f_recv, sib)
-
-    z_done(0)
-    send_all(0, NX, GROUP)
-    send_all(1, 1, GROUP)
-    y_round(0)
-    y_round(1)
-    z_done(1)
-    y_round(2)
-    y_round(3)
-    z_done(2)
-    y_round(4)
-    head_pass(0, {2: lambda: y_round(5), 5: lambda: y_round(6)})
-    y_round(7)
-    y_round(8)
-    x_done(0, 0)
-    x_done(1, 0)
-    y_round(9)
-    head_pass(1, {2: lambda: y_round(10), 5: lambda: y_round(11)})
-    x_done(0, 1)
-    x_done(1, 1)
-    o_landed(0)
-    forward(0).start()
-    y_round(12)
-    x_done(1, 2)
-    o_landed(1)
-    forward(1).start()
-    y_round(13)
-    x_done(0, 2)
-    x_done(1, 3)
+        return remote(view, view, f_send, f_recv.at[slot], sib)
+
+    take(0)
+    lax.fori_loop(0, SLOTS * NTILES, part_of_heads, 0)
     r_local.wait()
     r_sib.wait_recv()
     g_sib.wait_recv()
-    all_landed(ob.at[:, 0], f_recv)
 
     wide = outv.shape[3]
     parts = outv.shape[0]
@@ -343,12 +344,12 @@
     per_zh = per_slot // NZ_HI
     depth = per_zh * wb.shape[1]
 
-    def products(pair, cols):
+    def products(slots, places, cols):
         acc = None
-        for j in pair:
+        for j in places:
             zh = orders[j]
             feats = pl.ds(pl.multiple_of(zh * depth, 128), depth)
-            for slot in range(SLOTS):
+            for slot in slots:
                 part = jnp.dot(
                     ob[slot, :, :, feats].reshape(NCORE * tok, depth),
                     wb[pl.ds(slot * per_slot + zh * per_zh, per_zh), :, cols].reshape(depth, wide),
@@ -358,12 +359,16 @@
         return acc
 
     def early(n, _):
-        sums[n] = products((0, 1), pl.ds(pl.multiple_of(n * wide, 128), wide))
+        sums[n] = products((0,), (0, 1), pl.ds(pl.multiple_of(n * wide, 128), wide))
+        return 0
+
+    def middle(n, _):
+        sums[n] += products((1,), (0, 1), pl.ds(pl.multiple_of(n * wide, 128), wide))
         return 0
 
     def late(n, _):
         cols = pl.ds(pl.multiple_of(n * wide, 128), wide)
-        acc = sums[n] + products((2, 3), cols)
+        acc = sums[n] + products((0, 1), (2, 3), cols)
         for clip in range(NCORE):
             rows = acc[clip * tok : (clip + 1) * tok]
             mixed = rb[clip, :, cols].astype(jnp.float32) + gb[clip, 0:1, cols] * rows
@@ -374,7 +379,12 @@
 
     half_far = NCORE * NZ_HI * (NY - 1) // 2
     all_landed(wb.at[0:half_far, :, 0:SHARED], b_recv.at[0])
+    all_landed(ob.at[0, 0], f_recv.at[0])
     lax.fori_loop(0, parts, early, 0)
+    o_landed(1)
+    forward(1).start()
+    all_landed(ob.at[0, 0], f_recv.at[1])
+    lax.fori_loop(0, parts, middle, 0)
     all_landed(wb.at[0:half_far, :, 0:SHARED], b_recv.at[1])
     lax.fori_loop(0, parts, late, 0)
 
@@ -431,7 +441,7 @@
             dma((SLOTS,)),
             dma((SLOTS,)),
             dma,
-            dma,
+            dma((SLOTS,)),
             dma,
             dma((shards,)),
             dma,

time: 75.3 us -> 71.1 us (0.944)
  Pallas kernels: 72.7 us -> 68.5 us
    pallas_call x1, Pallas kernels: 72.7 us -> 68.5 us  [on_device(): pl.pallas_call(kernel, out_shape=jax.ShapeDtypeStruct(residual.shape, res...]
where the time goes in v3:
time: 71.1 us; the launch traced here: 70.9 us
  Pallas kernels  68.5 us (96%)
  local copies, waits for them, and re-layouts  2.36 us (3%)
    pallas_call x1, Pallas kernels, on_device(): pl.pallas_call(kernel, out_shape=jax.ShapeDtypeStruct(residual.shape, res...  68.5 us
    unnamed x1, local copies, waits for them, and re-layouts  2.36 us

profile of v3, /device:TPU:1, one launch (start us, length us, event | category | flops | bytes accessed | tf_op | source)
XLA Modules:
  0.0 70.9 jit_solution(14607365500295691950)
XLA Ops:
  0.0 68.5 %shard_map.82 = bf16[1,192,3072]{2,1,0:T(8,128)(2,1)} custom-call(bf16[1,192,2048]{2,1,0:T(8,128)(2,1)} %q_in.1, bf16[1,192,2048]{2,1,0:T(8,128)(2,1)} %k_in.1, bf16[1,192,2048]{2,1,0:T(8,128)(2,1)} %v_in.1, s32[4,4,16]{2,1,0:T(4,128)} %bitcast.2, s32[4,16]{1,0:T(4,128)} %bitcast.3, bf16[32,3072]{1,0:T(8,128)(2,1)} %w_in.1, bf16[1,3072]{1,0:T(2,128)(2,1)} %gate_in.1, ...), custom_call_target="tpu_custom_call" | custom-call | tf_op jit(solution)/shard_map/pallas_call | solution.py:420
  68.5 2.4 %copy.10 = bf16[1,192,3072]{2,1,0:T(8,128)(2,1)} copy(bf16[1,192,3072]{2,1,0:T(8,128)(2,1)} %shard_map.82) | data formatting | bytes 2359296

commit v4 on v3

--- a/solution.py
+++ b/solution.py
@@ -18,12 +18,13 @@
 NTILES = 4
 SHARED = 384
 STEPS = ((4, 3, 4, 3), (3, 4, 3, 4))
+LAST = 0
 BESIDE = 1
 ORDER = (
-    (("y", 0, 0, 0, 0), ("y", 1, 0, 0, 0), ("z", 0, 0), ("y", 0, 0, 1, 0), ("y", 1, 0, 1, 0), ("z", 0, 1),
-     ("y", 0, 0, 0, 1), ("y", 1, 0, 0, 1), ("z", 1, 0), ("y", 0, 1, 0, 0), ("y", 1, 1, 0, 0), ("z", 1, 1),
-     ("y", 0, 0, 1, 1), ("y", 1, 0, 1, 1), ("y", 0, 0, 0, 2), ("y", 1, 0, 0, 2), ("z", 2, 0),
-     ("y", 0, 2, 0, 0), ("y", 1, 2, 0, 0), ("y", 0, 1, 0, 1), ("y", 1, 1, 0, 1), ("z", 2, 1),
+    (("y", 0, 0, 0, 0), ("y", 1, 0, 0, 0), ("z", 0, 0), ("y", 0, 0, 1, 0), ("y", 1, 0, 1, 0), ("z", 0, 1), ("f", 1, 0),
+     ("y", 0, 0, 0, 1), ("y", 1, 0, 0, 1), ("z", 1, 0), ("f", 2, 0), ("y", 0, 1, 0, 0), ("y", 1, 1, 0, 0), ("z", 1, 1), ("f", 2, 1),
+     ("y", 0, 0, 1, 1), ("y", 1, 0, 1, 1), ("y", 0, 0, 0, 2), ("y", 1, 0, 0, 2), ("z", 2, 0), ("f", 3, 0),
+     ("y", 0, 2, 0, 0), ("y", 1, 2, 0, 0), ("y", 0, 1, 0, 1), ("y", 1, 1, 0, 1), ("z", 2, 1), ("f", 3, 1),
      ("y", 0, 2, 1, 0), ("y", 1, 2, 1, 0), ("y", 0, 0, 1, 2), ("y", 1, 0, 1, 2),),
     (("y", 0, 0, 0, 3), ("y", 1, 3, 0, 0),),
     (("y", 0, 3, 0, 0), ("y", 1, 2, 0, 1),),
@@ -40,10 +41,10 @@
 
 
 def kernel(
-    q_in, k_in, v_in, tiles, counts, w_in, gate_in, res_in, out,
-    qb, kb, vb, stage, ob, wb, rb, gs, gb, sums, outv,
+    q_in, k_in, v_in, tiles_in, counts_in, w_in, gate_in, res_in, out,
+    tiles, counts, qb, kb, vb, stage, ob, wb, rb, gs, gb, outv,
     a_send, a_recv, a_loc, o_send, o_recv, o_loc, f_send, f_recv, y_send, y_recv, x_send, x_recv,
-    b_send, b_recv, z_send, z_recv, s_send, s_recv, s_loc, p_send, p_recv, p_loc,
+    b_send, b_recv, z_send, z_recv, s_send, s_recv, s_loc, t_loc, p_send, p_recv, p_loc,
 ):
     dp, me = lax.axis_index("dp"), lax.axis_index("seq")
     z_hi, y, core = dp // (NY * NCORE), (dp // NCORE) % NY, dp % NCORE
@@ -95,6 +96,15 @@
     b_cols_in = pl.ds(pl.multiple_of((1 - z_lo) * (half - SHARED), 128), SHARED)
     own_shard = shard_at(z_hi, y, 0)
 
+    barrier = pltpu.get_barrier_semaphore()
+    for to in (sib, *ring, near):
+        pl.semaphore_signal(barrier, inc=1, device_id=to, device_id_type=MESH)
+
+    def greet(i, _):
+        pl.semaphore_signal(barrier, inc=1, device_id=(dp, peer(i)), device_id_type=MESH)
+        return 0
+
+    lax.fori_loop(1, GROUP, greet, 0)
     w_local = pltpu.make_async_copy(
         w_in.at[:, mine], wb.at[own_shard], s_loc.at[0]
     )
@@ -108,21 +118,16 @@
     for slot in range(SLOTS):
         for n in range(3):
             own_copy(n, slot).start()
+    t_local = pltpu.make_async_copy(tiles_in, tiles, t_loc.at[0])
+    c_local = pltpu.make_async_copy(counts_in, counts, t_loc.at[1])
+    t_local.start()
+    c_local.start()
     r_local = pltpu.make_async_copy(res_in.at[0, :, mine], rb.at[core], s_loc.at[1])
     r_local.start()
     gs[...] = jnp.broadcast_to(gate_in[...].astype(jnp.float32), gs.shape)
     g_local = pltpu.make_async_copy(gs.at[:, mine], gb.at[core], s_loc.at[2])
     g_local.start()
 
-    barrier = pltpu.get_barrier_semaphore()
-    for to in (sib, *ring, near):
-        pl.semaphore_signal(barrier, inc=1, device_id=to, device_id_type=MESH)
-
-    def greet(i, _):
-        pl.semaphore_signal(barrier, inc=1, device_id=(dp, peer(i)), device_id_type=MESH)
-        return 0
-
-    lax.fori_loop(1, GROUP, greet, 0)
     pl.semaphore_wait(barrier, GROUP + 3)
 
     w_sib = remote(
@@ -165,16 +170,14 @@
         view = wb.at[at, :, y_cols]
         return remote(view, view, x_send, x_recv.at[way, t], beside[way])
 
-    def b_copy(j, at):
+    def b_copy(at):
         view = wb.at[at, :, b_cols]
-        return remote(view, view, b_send, b_recv.at[j // 2], near)
+        return remote(view, view, b_send, b_recv, near)
 
     def shard_of(j, yy, part):
         return shard_at(orders[j], yy, kept if j == BESIDE else part)
 
     def y_first(j, part):
-        if j == BESIDE and part:
-            return
         at = shard_of(j, y, part)
         for way in range(2):
             y_copy(way, at).start()
@@ -189,29 +192,25 @@
             y_copy(way, at).start()
         if j == BESIDE:
             x_copy(way, t, at).start()
-        b_copy(j, at).start()
+        b_copy(at).start()
 
     def x_done(way, t):
         at = shard_at(orders[BESIDE], row_of(way, t), skipped)
         x_copy(way, t, at).wait_recv()
-        b_copy(BESIDE, at).start()
+        b_copy(at).start()
 
     def z_done(n, part):
         z_arrival(n, part).wait_recv()
         if n < 2:
             z_copy(n + 1, part).start()
-        if n + 1 != BESIDE:
-            y_first(n + 1, part)
-        elif part:
-            y_first(n + 1, 0)
         if n == 0 and part:
             send_all(0, NX, GROUP)
             send_all(1, 1, GROUP)
 
-    steps = {"z": z_done, "y": y_done, "x": x_done}
+    steps = {"f": y_first, "z": z_done, "y": y_done, "x": x_done}
 
     def take(group):
-        for name, *where in ORDER[group]:
+        for name, *where in group:
             steps[name](*where)
 
     w_local.wait()
@@ -307,10 +306,8 @@
             def _(group=group):
                 if group % NTILES == 0:
                     o_own(group // NTILES).start()
-                if group == SLOTS * NTILES - 1:
-                    o_landed(0)
-                    forward(0).start()
-                take(group + 1)
+                if group < SLOTS * NTILES - 1:
+                    take(ORDER[group + 1])
 
         return 0
 
@@ -320,13 +317,23 @@
 
     def forward(slot):
         view = ob.at[slot, core]
-        return remote(view, view, f_send, f_recv.at[slot], sib)
-
-    take(0)
+        return remote(view, view, f_send, f_recv, sib)
+
+    take(ORDER[0])
+    t_local.wait()
+    c_local.wait()
     lax.fori_loop(0, SLOTS * NTILES, part_of_heads, 0)
+    o_landed(0)
+    forward(0).start()
+    last = len(ORDER[-1]) - LAST
+    take(ORDER[-1][:last])
+    o_landed(1)
+    forward(1).start()
+    take(ORDER[-1][last:])
     r_local.wait()
     r_sib.wait_recv()
     g_sib.wait_recv()
+    all_landed(ob.at[0:2, 0], f_recv)
 
     wide = outv.shape[3]
     parts = outv.shape[0]
@@ -341,34 +348,19 @@
         return remote(outv.at[n, other], out.at[0, :, out_cols(n)], p_send, p_recv, sib)
 
     per_slot = wb.shape[0] // SLOTS
-    per_zh = per_slot // NZ_HI
-    depth = per_zh * wb.shape[1]
-
-    def products(slots, places, cols):
+    depth = per_slot * wb.shape[1]
+
+    def project(i, _):
+        n = (i + z_lo) % parts
+        cols = pl.ds(pl.multiple_of(n * wide, 128), wide)
         acc = None
-        for j in places:
-            zh = orders[j]
-            feats = pl.ds(pl.multiple_of(zh * depth, 128), depth)
-            for slot in slots:
-                part = jnp.dot(
-                    ob[slot, :, :, feats].reshape(NCORE * tok, depth),
-                    wb[pl.ds(slot * per_slot + zh * per_zh, per_zh), :, cols].reshape(depth, wide),
-                    preferred_element_type=jnp.float32,
-                )
-                acc = part if acc is None else acc + part
-        return acc
-
-    def early(n, _):
-        sums[n] = products((0,), (0, 1), pl.ds(pl.multiple_of(n * wide, 128), wide))
-        return 0
-
-    def middle(n, _):
-        sums[n] += products((1,), (0, 1), pl.ds(pl.multiple_of(n * wide, 128), wide))
-        return 0
-
-    def late(n, _):
-        cols = pl.ds(pl.multiple_of(n * wide, 128), wide)
-        acc = sums[n] + products((0, 1), (2, 3), cols)
+        for slot in range(SLOTS):
+            part = jnp.dot(
+                ob[slot].reshape(NCORE * tok, depth),
+                wb[slot * per_slot : (slot + 1) * per_slot, :, cols].reshape(depth, wide),
+                preferred_element_type=jnp.float32,
+            )
+            acc = part if acc is None else acc + part
         for clip in range(NCORE):
             rows = acc[clip * tok : (clip + 1) * tok]
             mixed = rb[clip, :, cols].astype(jnp.float32) + gb[clip, 0:1, cols] * rows
@@ -377,25 +369,25 @@
         out_sib(n).start()
         return 0
 
-    half_far = NCORE * NZ_HI * (NY - 1) // 2
-    all_landed(wb.at[0:half_far, :, 0:SHARED], b_recv.at[0])
-    all_landed(ob.at[0, 0], f_recv.at[0])
-    lax.fori_loop(0, parts, early, 0)
-    o_landed(1)
-    forward(1).start()
-    all_landed(ob.at[0, 0], f_recv.at[1])
-    lax.fori_loop(0, parts, middle, 0)
-    all_landed(wb.at[0:half_far, :, 0:SHARED], b_recv.at[1])
-    lax.fori_loop(0, parts, late, 0)
+    far = NCORE * NZ_HI * (NY - 1)
+
+    def project_in_turn(i, _):
+        @pl.when(i == parts - 1)
+        def _():
+            all_landed(wb.at[0:far, :, 0:SHARED], b_recv)
+
+        return project(i, 0)
+
+    lax.fori_loop(0, parts, project_in_turn, 0)
 
     for n in range(3):
         all_sent(kb.at[0:2, 0 : GROUP - 1], a_send.at[n])
     all_sent(stage.at[0:2, 0 : GROUP - 1], o_send)
-    all_sent(ob.at[:, 0], f_send)
+    all_sent(ob.at[0:2, 0], f_send)
     all_sent(wb.at[0 : 3 * NCORE], z_send)
     all_sent(wb.at[0 : (NCORE * NZ_HI - 1) * (NY - 1), :, 0 : half - SHARED], y_send)
     all_sent(wb.at[0 : NY - 1, :, 0 : half - SHARED], x_send)
-    all_sent(wb.at[0 : 2 * half_far, :, 0:SHARED], b_send)
+    all_sent(wb.at[0:far, :, 0:SHARED], b_send)
     w_sib.wait_send()
     r_sib.wait_send()
     g_sib.wait_send()
@@ -404,25 +396,46 @@
     all_landed(outv.at[:, 0], p_recv)
 
 
+def hand_over(strips, block, out, held, in_sem, out_sem):
+    rows = block.shape[1] // strips
+    copies = []
+    for n in range(strips):
+        part = (0, pl.ds(n * rows, rows))
+        copies.append(
+            (
+                pltpu.make_async_copy(block.at[part], held.at[part], in_sem.at[n]),
+                pltpu.make_async_copy(held.at[part], out.at[part], out_sem.at[n]),
+            )
+        )
+    for load, _ in copies:
+        load.start()
+    for load, store in copies:
+        load.wait()
+        store.start()
+    for _, store in copies:
+        store.wait()
+
+
 def on_device(
     query_rows, key_rows, value_rows, key_tiles, tile_counts, out_weight, gate_scale, residual
 ):
     tok, feats = query_rows.shape[1:]
     w_rows, width = out_weight.shape
     half = width // NCORE
-    parts = 6
+    parts = half // SHARED
     bf16, f32 = jnp.bfloat16, jnp.float32
     dma = pltpu.SemaphoreType.DMA
     shards = NZ_HI * NY * NCORE
     hbm = pl.BlockSpec(memory_space=pltpu.HBM)
-    smem = pl.BlockSpec(memory_space=pltpu.SMEM)
     vmem = pl.BlockSpec(memory_space=pltpu.VMEM)
-    return pl.pallas_call(
+    block_out = pl.pallas_call(
         kernel,
         out_shape=jax.ShapeDtypeStruct(residual.shape, residual.dtype),
-        in_specs=[hbm, hbm, hbm, smem, smem, hbm, vmem, hbm],
+        in_specs=[hbm, hbm, hbm, hbm, hbm, hbm, vmem, hbm],
         out_specs=pl.BlockSpec(memory_space=pl.ANY),
         scratch_shapes=[
+            pltpu.SMEM((NTILES, NTILES, feats // HEAD_DIM), jnp.int32),
+            pltpu.SMEM((NTILES, feats // HEAD_DIM), jnp.int32),
             pltpu.VMEM((SLOTS, GROUP, tok, HEAD_DIM), bf16),
             pltpu.VMEM((SLOTS, GROUP, tok, HEAD_DIM), bf16),
             pltpu.VMEM((SLOTS, GROUP, tok, HEAD_DIM), bf16),
@@ -432,7 +445,6 @@
             pltpu.VMEM((NCORE, tok, half), bf16),
             pltpu.VMEM((8, width), f32),
             pltpu.VMEM((NCORE, 8, half), f32),
-            pltpu.VMEM((parts, NCORE * tok, half // parts), f32),
             pltpu.VMEM((parts, NCORE, tok, half // parts), bf16),
             dma((3,)),
             dma((SLOTS, 3)),
@@ -441,18 +453,19 @@
             dma((SLOTS,)),
             dma((SLOTS,)),
             dma,
-            dma((SLOTS,)),
+            dma,
             dma,
             dma((shards,)),
             dma,
             dma((2, 4)),
             dma,
-            dma((2,)),
+            dma,
             dma,
             dma((3, NCORE)),
             dma((3,)),
             dma((3,)),
             dma((3,)),
+            dma((2,)),
             dma,
             dma,
             dma,
@@ -464,6 +477,18 @@
         query_rows, key_rows, value_rows, jnp.transpose(key_tiles, (1, 2, 0)), tile_counts.T,
         out_weight, gate_scale, residual,
     )
+    strips = 4
+    return pl.pallas_call(
+        functools.partial(hand_over, strips),
+        out_shape=jax.ShapeDtypeStruct(residual.shape, residual.dtype),
+        in_specs=[hbm],
+        out_specs=pl.BlockSpec(memory_space=pl.ANY),
+        scratch_shapes=[
+            pltpu.VMEM(residual.shape, residual.dtype),
+            dma((strips,)),
+            dma((strips,)),
+        ],
+    )(block_out)
 
 
 def solution(mesh):

time: 71.1 us -> 69 us (0.970)
  local copies, waits for them, and re-layouts: 2.36 us -> 0 us
    unnamed x1 -> x0, local copies, waits for them, and re-layouts: 2.36 us -> none
    pallas_call x0 -> x1, Pallas kernels: none -> 2.04 us  [on_device(): pl.pallas_call(functools.partial(hand_over, strips), out_shape=jax.ShapeD...]
    pallas_call x1, Pallas kernels: 68.5 us -> 66.8 us  [on_device(): pl.pallas_call(kernel, out_shape=jax.ShapeDtypeStruct(residual.shape, res...]
where the time goes in v4:
time: 69 us; the launch traced here: 68.8 us
  Pallas kernels  68.8 us (100%)
    pallas_call x1, Pallas kernels, on_device(): pl.pallas_call(kernel, out_shape=jax.ShapeDtypeStruct(residual.shape, res...  66.8 us
    pallas_call x1, Pallas kernels, on_device(): pl.pallas_call(functools.partial(hand_over, strips), out_shape=jax.ShapeD...  2.04 us

profile of v4, /device:TPU:1, one launch (start us, length us, event | category | flops | bytes accessed | tf_op | source)
XLA Modules:
  0.0 68.8 jit_solution(1998061257812046836)
XLA Ops:
  0.0 66.8 %shard_map.82.block = bf16[1,192,3072]{2,1,0:T(8,128)(2,1)} custom-call(bf16[1,192,2048]{2,1,0:T(8,128)(2,1)} %q_in.1, bf16[1,192,2048]{2,1,0:T(8,128)(2,1)} %k_in.1, bf16[1,192,2048]{2,1,0:T(8,128)(2,1)} %v_in.1, s32[4,4,16]{2,1,0:T(4,128)} %bitcast.2, s32[4,16]{1,0:T(4,128)} %bitcast.3, bf16[32,3072]{1,0:T(8,128)(2,1)} %w_in.1, bf16[1,3072]{1,0:T(2,128)(2,1)} %gate_in.1, ...), custom_call_target="tpu_custom_call" | custom-call | tf_op jit(solution)/shard_map/pallas_call | solution.py:431
  66.8 2.0 %shard_map.83 = bf16[1,192,3072]{2,1,0:T(8,128)(2,1)} custom-call(bf16[1,192,3072]{2,1,0:T(8,128)(2,1)} %shard_map.82.block), custom_call_target="tpu_custom_call" | custom-call | tf_op jit(solution)/shard_map/pallas_call | solution.py:481

commit v5 on v4

--- a/solution.py
+++ b/solution.py
@@ -16,7 +16,7 @@
 GROUP = NX * NZ_LO
 SLOTS = 2
 NTILES = 4
-SHARED = 384
+SHARED = (384, 384)
 STEPS = ((4, 3, 4, 3), (3, 4, 3, 4))
 LAST = 0
 BESIDE = 1
@@ -42,7 +42,7 @@
 
 def kernel(
     q_in, k_in, v_in, tiles_in, counts_in, w_in, gate_in, res_in, out,
-    tiles, counts, qb, kb, vb, stage, ob, wb, rb, gs, gb, outv,
+    tiles, counts, qb, kb, vb, stage, ob, wb, rb, gs, gb, sums, outv,
     a_send, a_recv, a_loc, o_send, o_recv, o_loc, f_send, f_recv, y_send, y_recv, x_send, x_recv,
     b_send, b_recv, z_send, z_recv, s_send, s_recv, s_loc, t_loc, p_send, p_recv, p_loc,
 ):
@@ -91,9 +91,8 @@
     orders = tuple(
         (z_hi + NZ_HI + off) % NZ_HI for off in (0, way_z, -way_z, 2)
     )
-    y_cols = pl.ds(pl.multiple_of(z_lo * SHARED, 128), half - SHARED)
-    b_cols = pl.ds(pl.multiple_of(z_lo * (half - SHARED), 128), SHARED)
-    b_cols_in = pl.ds(pl.multiple_of((1 - z_lo) * (half - SHARED), 128), SHARED)
+    y_cols = [pl.ds(pl.multiple_of(z_lo * n, 128), half - n) for n in SHARED]
+    b_cols = [pl.ds(pl.multiple_of(z_lo * (half - n), 128), n) for n in SHARED]
     own_shard = shard_at(z_hi, y, 0)
 
     barrier = pltpu.get_barrier_semaphore()
@@ -162,17 +161,17 @@
         view = wb.at[shard_at(orders[n + 1], y, part)]
         return remote(view, view, z_send, z_recv.at[n, part], (near, twin, near)[n])
 
-    def y_copy(way, at):
-        view = wb.at[at, :, y_cols]
-        return remote(view, view, y_send, y_recv.at[at], ring[way])
+    def y_copy(way, j, at):
+        view = wb.at[at, :, y_cols[j // 2]]
+        return remote(view, view, y_send.at[j // 2], y_recv.at[at], ring[way])
 
     def x_copy(way, t, at):
-        view = wb.at[at, :, y_cols]
+        view = wb.at[at, :, y_cols[BESIDE // 2]]
         return remote(view, view, x_send, x_recv.at[way, t], beside[way])
 
-    def b_copy(at):
-        view = wb.at[at, :, b_cols]
-        return remote(view, view, b_send, b_recv, near)
+    def b_copy(j, at):
+        view = wb.at[at, :, b_cols[j // 2]]
+        return remote(view, view, b_send.at[j // 2], b_recv.at[j // 2], near)
 
     def shard_of(j, yy, part):
         return shard_at(orders[j], yy, kept if j == BESIDE else part)
@@ -180,24 +179,24 @@
     def y_first(j, part):
         at = shard_of(j, y, part)
         for way in range(2):
-            y_copy(way, at).start()
+            y_copy(way, j, at).start()
 
     def row_of(way, t):
         return (y + ((NY - 1 - t) if way == 0 else t + 1)) % NY
 
     def y_done(way, j, part, t):
         at = shard_of(j, row_of(way, t), part)
-        y_copy(way, at).wait_recv()
+        y_copy(way, j, at).wait_recv()
         if t + 1 < STEPS[way][j]:
-            y_copy(way, at).start()
+            y_copy(way, j, at).start()
         if j == BESIDE:
             x_copy(way, t, at).start()
-        b_copy(at).start()
+        b_copy(j, at).start()
 
     def x_done(way, t):
         at = shard_at(orders[BESIDE], row_of(way, t), skipped)
         x_copy(way, t, at).wait_recv()
-        b_copy(at).start()
+        b_copy(BESIDE, at).start()
 
     def z_done(n, part):
         z_arrival(n, part).wait_recv()
@@ -350,9 +349,23 @@
     per_slot = wb.shape[0] // SLOTS
     depth = per_slot * wb.shape[1]
 
+    per_zh = per_slot // NZ_HI
+    zh_depth = per_zh * wb.shape[1]
+
+    def out_cols_at(i):
+        n = (i + z_lo) % parts
+        return n, pl.ds(pl.multiple_of(n * wide, 128), wide)
+
+    def finish(n, cols, acc):
+        for clip in range(NCORE):
+            rows = acc[clip * tok : (clip + 1) * tok]
+            mixed = rb[clip, :, cols].astype(jnp.float32) + gb[clip, 0:1, cols] * rows
+            outv[n, clip] = mixed.astype(jnp.bfloat16)
+        out_own(n).start()
+        out_sib(n).start()
+
     def project(i, _):
-        n = (i + z_lo) % parts
-        cols = pl.ds(pl.multiple_of(n * wide, 128), wide)
+        n, cols = out_cols_at(i)
         acc = None
         for slot in range(SLOTS):
             part = jnp.dot(
@@ -361,33 +374,42 @@
                 preferred_element_type=jnp.float32,
             )
             acc = part if acc is None else acc + part
-        for clip in range(NCORE):
-            rows = acc[clip * tok : (clip + 1) * tok]
-            mixed = rb[clip, :, cols].astype(jnp.float32) + gb[clip, 0:1, cols] * rows
-            outv[n, clip] = mixed.astype(jnp.bfloat16)
-        out_own(n).start()
-        out_sib(n).start()
+        finish(n, cols, acc)
         return 0
 
-    far = NCORE * NZ_HI * (NY - 1)
-
-    def project_in_turn(i, _):
-        @pl.when(i == parts - 1)
-        def _():
-            all_landed(wb.at[0:far, :, 0:SHARED], b_recv)
-
-        return project(i, 0)
-
-    lax.fori_loop(0, parts, project_in_turn, 0)
+    def products(places, cols):
+        acc = None
+        for j in places:
+            zh = orders[j]
+            feats = pl.ds(pl.multiple_of(zh * zh_depth, 128), zh_depth)
+            for slot in range(SLOTS):
+                part = jnp.dot(
+                    ob[slot, :, :, feats].reshape(NCORE * tok, zh_depth),
+                    wb[pl.ds(slot * per_slot + zh * per_zh, per_zh), :, cols].reshape(zh_depth, wide),
+                    preferred_element_type=jnp.float32,
+                )
+                acc = part if acc is None else acc + part
+        return acc
+
+    far = NCORE * NZ_HI * (NY - 1) // 2
+    all_landed(wb.at[0:far, :, 0 : SHARED[0]], b_recv.at[0])
+
+    lax.fori_loop(0, parts - 1, project, 0)
+    last_n, last_cols = out_cols_at(parts - 1)
+    sums[...] = products((0, 1), last_cols)
+    all_landed(wb.at[0:far, :, 0 : SHARED[1]], b_recv.at[1])
+    finish(last_n, last_cols, sums[...] + products((2, 3), last_cols))
 
     for n in range(3):
         all_sent(kb.at[0:2, 0 : GROUP - 1], a_send.at[n])
     all_sent(stage.at[0:2, 0 : GROUP - 1], o_send)
     all_sent(ob.at[0:2, 0], f_send)
     all_sent(wb.at[0 : 3 * NCORE], z_send)
-    all_sent(wb.at[0 : (NCORE * NZ_HI - 1) * (NY - 1), :, 0 : half - SHARED], y_send)
-    all_sent(wb.at[0 : NY - 1, :, 0 : half - SHARED], x_send)
-    all_sent(wb.at[0:far, :, 0:SHARED], b_send)
+    for n in range(2):
+        taken = far - (NY - 1) * (n == BESIDE // 2)
+        all_sent(wb.at[0:taken, :, 0 : half - SHARED[n]], y_send.at[n])
+        all_sent(wb.at[0:far, :, 0 : SHARED[n]], b_send.at[n])
+    all_sent(wb.at[0 : NY - 1, :, 0 : half - SHARED[BESIDE // 2]], x_send)
     w_sib.wait_send()
     r_sib.wait_send()
     g_sib.wait_send()
@@ -422,7 +444,7 @@
     tok, feats = query_rows.shape[1:]
     w_rows, width = out_weight.shape
     half = width // NCORE
-    parts = half // SHARED
+    parts = half // SHARED[1]
     bf16, f32 = jnp.bfloat16, jnp.float32
     dma = pltpu.SemaphoreType.DMA
     shards = NZ_HI * NY * NCORE
@@ -445,6 +467,7 @@
             pltpu.VMEM((NCORE, tok, half), bf16),
             pltpu.VMEM((8, width), f32),
             pltpu.VMEM((NCORE, 8, half), f32),
+            pltpu.VMEM((NCORE * tok, half // parts), f32),
             pltpu.VMEM((parts, NCORE, tok, half // parts), bf16),
             dma((3,)),
             dma((SLOTS, 3)),
@@ -454,12 +477,12 @@
             dma((SLOTS,)),
             dma,
             dma,
-            dma,
+            dma((2,)),
             dma((shards,)),
             dma,
             dma((2, 4)),
-            dma,
-            dma,
+            dma((2,)),
+            dma((2,)),
             dma,
             dma((3, NCORE)),
             dma((3,)),

time: 69 us -> 69.1 us (level)
  no operation moved by 1% of the time
where the time goes in v5:
time: 69.1 us; the launch traced here: 68.9 us
  Pallas kernels  68.9 us (100%)
    pallas_call x1, Pallas kernels, on_device(): pl.pallas_call(kernel, out_shape=jax.ShapeDtypeStruct(residual.shape, res...  66.8 us
    pallas_call x1, Pallas kernels, on_device(): pl.pallas_call(functools.partial(hand_over, strips), out_shape=jax.ShapeD...  2.04 us

profile of v5, /device:TPU:1, one launch (start us, length us, event | category | flops | bytes accessed | tf_op | source)
XLA Modules:
  0.0 68.9 jit_solution(14552332424380122816)
XLA Ops:
  0.0 66.8 %shard_map.82.block = bf16[1,192,3072]{2,1,0:T(8,128)(2,1)} custom-call(bf16[1,192,2048]{2,1,0:T(8,128)(2,1)} %q_in.1, bf16[1,192,2048]{2,1,0:T(8,128)(2,1)} %k_in.1, bf16[1,192,2048]{2,1,0:T(8,128)(2,1)} %v_in.1, s32[4,4,16]{2,1,0:T(4,128)} %bitcast.2, s32[4,16]{1,0:T(4,128)} %bitcast.3, bf16[32,3072]{1,0:T(8,128)(2,1)} %w_in.1, bf16[1,3072]{1,0:T(2,128)(2,1)} %gate_in.1, ...), custom_call_target="tpu_custom_call" | custom-call | tf_op jit(solution)/shard_map/pallas_call | solution.py:453
  66.9 2.0 %shard_map.83 = bf16[1,192,3072]{2,1,0:T(8,128)(2,1)} custom-call(bf16[1,192,3072]{2,1,0:T(8,128)(2,1)} %shard_map.82.block), custom_call_target="tpu_custom_call" | custom-call | tf_op jit(solution)/shard_map/pallas_call | solution.py:504
